TPU v7x, 32 devices: a whole 2x2x4 slice. The times are simulated.
32 devices in a mesh: dp: 8 (over z, x), tensor: 4 (over y, core).
Axes of the slice: x: 2, y: 2, z: 4, core: 2. Of those that a mesh axis runs over, the one named last changes fastest.
Arguments:
- tokens: bfloat16 [2048, 2048], P(('dp', 'tensor')), may hold values from -6 to 6
- grad_out: bfloat16 [2048, 2048], P(('dp', 'tensor')), may hold values from -6 to 6
- lengths: int32 [8, 3], P('dp'), may hold values from 1 to 254, as said below
- gain_attn: bfloat16 [2048], P('dp'), may hold values from 0.5 to 1.5
- gain_ffn: bfloat16 [2048], P('dp'), may hold values from 0.5 to 1.5
- w_query: bfloat16 [2048, 2048], P('dp', 'tensor'), may hold values from -0.125 to 0.125
- w_keyval: bfloat16 [2048, 512], P('dp'), may hold values from -0.125 to 0.125
- w_out: bfloat16 [2048, 2048], P('dp', 'tensor'), may hold values from -1 to 1
- w_gate: bfloat16 [2048, 16384], P('dp', 'tensor'), may hold values from -0.125 to 0.125
- w_up: bfloat16 [2048, 16384], P('dp', 'tensor'), may hold values from -0.125 to 0.125
- w_down: bfloat16 [2048, 16384], P('dp', 'tensor'), may hold values from -0.046875 to 0.046875
Outputs:
- block_out: bfloat16 [2048, 2048], P(('dp', 'tensor'))
- grad_tokens: float32 [2048, 2048], P(('dp', 'tensor'))
- grad_gain_attn: float32 [2048], P('dp')
- grad_gain_ffn: float32 [2048], P('dp')
- grad_w_query: float32 [2048, 2048], P('dp', 'tensor')
- grad_w_keyval: float32 [2048, 512], P('dp')
- grad_w_out: float32 [2048, 2048], P('dp', 'tensor')
- grad_w_gate: float32 [2048, 16384], P('dp', 'tensor')
- grad_w_up: float32 [2048, 16384], P('dp', 'tensor')
- grad_w_down: float32 [2048, 16384], P('dp', 'tensor')
Inputs may be any that keep to these rules, and one draw needn't show every extreme that they name: Each row of lengths holds the lengths of the 3 sequences of one group in order and sums to 256; in every group one sequence, at a position drawn from the seed, begins before place 64 - 1 and ends after place 3 * 64.
All inputs are finite; a program needn't handle non-finite values.
Results may differ from a plain program's by a relative error of at most 0.024.
Values may be sent and summed in bfloat16 or wider, within the bound.
A program may use at most 320 MiB of HBM per device.

v0:
```python
import jax
import jax.numpy as jnp
from jax import lax
from jax.sharding import PartitionSpec as P

HD = 256
WINDOW = 2048


norm_eps = 1e-06
masked_score = -1e30


def as_sent(value):

    def short(part):
        return part.astype(jnp.bfloat16) if part.dtype == jnp.float32 else part

    return jax.tree.map(short, value)


def norm_rows(values_in, gain_vec):
    inverse_root = lax.rsqrt(jnp.mean(values_in * values_in, axis=-1, keepdims=True) + norm_eps)
    return values_in * inverse_root * gain_vec


def gelu_mix(gate_act, up_act):
    return jax.nn.gelu(gate_act, approximate=True) * up_act


def segment_ids(length_row, row_count):
    seq_ends = jnp.cumsum(length_row)
    positions = jnp.arange(row_count, dtype=jnp.int32)
    return jnp.sum((positions[:, None] >= seq_ends[None, :]).astype(jnp.int32), axis=1)


def mul_last(left_mat, right_mat):
    return lax.dot_general(
        left_mat, right_mat, (((1,), (1,)), ((), ())), preferred_element_type=jnp.float32
    )


def mul_first(left_mat, right_mat):
    return lax.dot_general(
        left_mat, right_mat, (((0,), (0,)), ((), ())), preferred_element_type=jnp.float32
    )


def window_allowed(segment, block_start, block_rows):
    row_count = segment.shape[0]
    query_place = block_start + jnp.arange(block_rows, dtype=jnp.int32)
    key_place = jnp.arange(row_count, dtype=jnp.int32)
    distance = query_place[:, None] - key_place[None, :]
    return (segment[:, None] == segment[None, :]) & (distance >= 0) & (distance < WINDOW)


def block_scores(query_heads, keys_low, segment, block_start, block_rows):
    allowed = window_allowed(segment, block_start, block_rows)
    scores = jnp.einsum(
        "qhd,kd->hqk", query_heads, keys_low, preferred_element_type=jnp.float32
    ) * HD ** (-0.5)
    return (query_heads, jnp.where(allowed[None], scores, masked_score))


def attend_forward(queries, keyval, segment):
    row_count = queries.shape[0]
    heads_here = queries.shape[1] // HD
    query_heads = queries.reshape(row_count, heads_here, HD)
    keys_low = keyval[:, :HD]
    values_low = keyval[:, HD:]

    def one_block(block_index):
        block_start = block_index * row_count
        query_block, scores = block_scores(query_heads, keys_low, segment, block_start, row_count)
        peak_score = jnp.max(scores, axis=-1, keepdims=True)
        weights = jnp.exp(scores - peak_score)
        totals = jnp.sum(weights, axis=-1, keepdims=True)
        probs_low = (weights / totals).astype(jnp.bfloat16)
        context = jnp.einsum(
            "hqk,kd->qhd", probs_low, values_low, preferred_element_type=jnp.float32
        )
        return (context, (peak_score + jnp.log(totals))[..., 0])

    contexts, log_sums = lax.map(one_block, jnp.arange(row_count // row_count, dtype=jnp.int32))
    return (contexts.reshape(row_count, heads_here * HD).astype(jnp.bfloat16), log_sums)


def attend_backward(queries, keyval, segment, log_sums, grad_context):
    row_count = queries.shape[0]
    heads_here = queries.shape[1] // HD
    query_heads = queries.reshape(row_count, heads_here, HD)
    grad_heads = grad_context.reshape(row_count, heads_here, HD)
    keys_low = keyval[:, :HD]
    values_low = keyval[:, HD:]
    factor = HD ** (-0.5)

    def back_block(block_index):
        block_start = block_index * row_count
        query_block, scores = block_scores(query_heads, keys_low, segment, block_start, row_count)
        probabilities = jnp.exp(scores - log_sums[block_index][..., None])
        probs_low = probabilities.astype(jnp.bfloat16)
        grad_probs = jnp.einsum(
            "qhd,kd->hqk", grad_heads, values_low, preferred_element_type=jnp.float32
        )
        inner_sum = jnp.sum(grad_probs * probabilities, axis=-1, keepdims=True)
        grad_scores = (probabilities * (grad_probs - inner_sum)).astype(jnp.bfloat16)
        grad_query_block = (
            jnp.einsum("hqk,kd->qhd", grad_scores, keys_low, preferred_element_type=jnp.float32)
            * factor
        )
        grad_keys = (
            jnp.einsum("hqk,qhd->kd", grad_scores, query_block, preferred_element_type=jnp.float32)
            * factor
        )
        grad_values = jnp.einsum(
            "hqk,qhd->kd", probs_low, grad_heads, preferred_element_type=jnp.float32
        )
        return (grad_query_block, jnp.concatenate([grad_keys, grad_values], axis=1))

    grad_queries, grad_keyvals = lax.map(
        back_block, jnp.arange(row_count // row_count, dtype=jnp.int32)
    )
    grad_queries = grad_queries.reshape(row_count, heads_here * HD).astype(jnp.bfloat16)
    return (grad_queries, jnp.sum(grad_keyvals, axis=0))


def body(
    tokens, grad_out, lengths, gain_attn, gain_ffn, w_query, w_keyval, w_out, w_gate, w_up, w_down
):
    tensor_rank = lax.axis_index("tensor")
    own_rows = tokens.shape[0]
    group_tokens, cotangent = (
        lax.all_gather(tokens, "tensor", axis=0, tiled=True),
        lax.all_gather(grad_out, "tensor", axis=0, tiled=True),
    )
    total_rows = group_tokens.shape[0]
    own_start = tensor_rank * own_rows
    inputs = group_tokens.astype(jnp.float32)
    query_all, keyval_all, out_all, gain_one, gain_two = (
        lax.all_gather(w_query, "dp", axis=0, tiled=True),
        lax.all_gather(w_keyval, "dp", axis=0, tiled=True),
        lax.all_gather(w_out, "dp", axis=0, tiled=True),
        lax.all_gather(gain_attn, "dp", axis=0, tiled=True),
        lax.all_gather(gain_ffn, "dp", axis=0, tiled=True),
    )
    segment = segment_ids(lengths[0], total_rows)
    normed_one, norm_pull_one = jax.vjp(norm_rows, inputs, gain_one.astype(jnp.float32))
    normed_attn = normed_one.astype(jnp.bfloat16)
    queries = jnp.dot(normed_attn, query_all, preferred_element_type=jnp.float32).astype(
        jnp.bfloat16
    )
    keyval = jnp.dot(normed_attn, keyval_all, preferred_element_type=jnp.float32).astype(
        jnp.bfloat16
    )
    context, log_sums = attend_forward(queries, keyval, segment)
    branch = lax.psum(mul_last(context, out_all).astype(jnp.bfloat16), "tensor").astype(jnp.float32)
    middle = inputs + branch
    normed_two, norm_pull_two = jax.vjp(norm_rows, middle, gain_two.astype(jnp.float32))
    normed_ffn = normed_two.astype(jnp.bfloat16)
    pieces = (
        lax.all_gather(w_gate, "dp", axis=0, tiled=True),
        lax.all_gather(w_up, "dp", axis=0, tiled=True),
    )
    columns = normed_ffn
    gate_act = jnp.dot(columns, pieces[0], preferred_element_type=jnp.float32)
    up_act = jnp.dot(columns, pieces[1], preferred_element_type=jnp.float32)
    hidden = gelu_mix(gate_act, up_act).astype(jnp.bfloat16)
    ffn_term = mul_last(hidden, lax.all_gather(w_down, "dp", axis=0, tiled=True))
    ffn_own = lax.psum_scatter(
        ffn_term.astype(jnp.bfloat16), "tensor", scatter_dimension=0, tiled=True
    ).astype(jnp.float32)
    middle_own = lax.dynamic_slice_in_dim(middle, own_start, own_rows, 0)
    block_out = (middle_own + ffn_own).astype(jnp.bfloat16)
    columns = cotangent
    grad_hidden = jnp.dot(
        columns,
        lax.all_gather(w_down, "dp", axis=0, tiled=True),
        preferred_element_type=jnp.float32,
    )
    mix_out, mix_pull = jax.vjp(gelu_mix, gate_act, up_act)
    grad_gate_f, grad_up_f = mix_pull(grad_hidden)
    grad_gate = grad_gate_f.astype(jnp.bfloat16)
    grad_up = grad_up_f.astype(jnp.bfloat16)
    pieces = (
        lax.all_gather(w_gate, "dp", axis=0, tiled=True),
        lax.all_gather(w_up, "dp", axis=0, tiled=True),
    )
    term = mul_last(grad_gate, pieces[0]) + mul_last(grad_up, pieces[1])
    grad_normed_ffn = lax.psum(term.astype(jnp.bfloat16), "tensor").astype(jnp.float32)
    grad_middle_norm, grad_gain_two = norm_pull_two(grad_normed_ffn)
    grad_middle = cotangent.astype(jnp.float32) + grad_middle_norm
    grad_branch = grad_middle.astype(jnp.bfloat16)
    grad_context = jnp.dot(grad_branch, out_all, preferred_element_type=jnp.float32).astype(
        jnp.bfloat16
    )
    grad_queries, grad_keyval_part = attend_backward(
        queries, keyval, segment, log_sums, grad_context
    )
    query_partial = mul_last(grad_queries, query_all)
    query_sum, keyval_sum = (
        lax.psum(query_partial.astype(jnp.bfloat16), "tensor").astype(jnp.float32),
        lax.psum(grad_keyval_part.astype(jnp.bfloat16), "tensor").astype(jnp.float32),
    )
    grad_keyval = keyval_sum.astype(jnp.bfloat16)
    grad_normed_attn = query_sum + mul_last(grad_keyval, keyval_all)
    grad_input_norm, grad_gain_one = norm_pull_one(grad_normed_attn)
    grad_inputs = grad_middle + grad_input_norm
    grad_tokens = lax.dynamic_slice_in_dim(grad_inputs, own_start, own_rows, 0)
    attn_terms = (
        mul_first(normed_attn, grad_queries),
        mul_first(normed_attn, grad_keyval),
        mul_first(grad_branch, context),
    )
    ffn_terms = (
        mul_first(normed_ffn, grad_gate),
        mul_first(normed_ffn, grad_up),
        mul_first(cotangent, hidden),
    )
    grad_w_gate, grad_w_up, grad_w_down, grad_w_query, grad_w_keyval, grad_w_out = jax.tree.map(
        lambda part: part.astype(jnp.float32),
        lax.psum_scatter(as_sent(ffn_terms + attn_terms), "dp", scatter_dimension=0, tiled=True),
    )
    gain_attn_grad, gain_ffn_grad = (
        lax.psum_scatter(grad_gain_one, "dp", scatter_dimension=0, tiled=True),
        lax.psum_scatter(grad_gain_two, "dp", scatter_dimension=0, tiled=True),
    )
    return (
        block_out,
        grad_tokens,
        gain_attn_grad,
        gain_ffn_grad,
        grad_w_query,
        grad_w_keyval,
        grad_w_out,
        grad_w_gate,
        grad_w_up,
        grad_w_down,
    )


def solution(mesh):
    placed = (
        P(("dp", "tensor"), None),
        P(("dp", "tensor"), None),
        P("dp", None),
        P("dp"),
        P("dp"),
        P("dp", "tensor"),
        P("dp", None),
        P("dp", "tensor"),
        P("dp", "tensor"),
        P("dp", "tensor"),
        P("dp", "tensor"),
    )
    return jax.shard_map(
        body,
        mesh=mesh,
        in_specs=placed,
        out_specs=(
            P(("dp", "tensor"), None),
            P(("dp", "tensor"), None),
            P("dp"),
            P("dp"),
            P("dp", "tensor"),
            P("dp", None),
            P("dp", "tensor"),
            P("dp", "tensor"),
            P("dp", "tensor"),
            P("dp", "tensor"),
        ),
        check_vma=False,
    )
```

profile of v0, /device:TPU:0, one launch (start us, length us, event | category | flops | bytes accessed | tf_op | source)
XLA Modules:
  0.0 2160.8 jit_solution(18126971531959587129)
XLA Ops:
  10.7 22.2 %all-gather = bf16[8,1,256]{2,1,0:T(2,128)(2,1)S(1)} all-gather(bf16[1,1,256]{2,1,0:T(2,128)(2,1)S(1)} %reshape.166), channel_id=1, replica_groups=mesh['dp'=8,'tensor'=4] {'dp'}, dimensions={0}, use_global_device_ids=true | all-gather | bytes 4608 | tf_op jit(solution)/shard_map/all_gather | solution.py:143
  35.5 45.0 %all-gather.15.cloned.1.call-done = bf16[2048,512]{1,0:T(8,128)(2,1)} async-done(((bf16[256,512]{1,0:T(8,128)(2,1)}), bf16[2048,512]{1,0:T(8,128)(2,1)}) %all-gather.15.cloned.1.call-update) | async-done | bytes 2097168 | tf_op jit(solution)/shard_map/all_gather | solution.py:140
  80.5 2.7 convolution_convert_fusion.10
  83.4 47.0 %all-gather.13.cloned.1.call-done = bf16[2048,512]{1,0:T(8,128)(2,1)} async-done(((bf16[256,512]{1,0:T(8,128)(2,1)}), bf16[2048,512]{1,0:T(8,128)(2,1)}) %all-gather.13.cloned.1.call-update) | async-done | bytes 2097168 | tf_op jit(solution)/shard_map/all_gather | solution.py:141
  130.4 2.3 convolution_convert_fusion.11
  134.1 46.1 %all-gather.17.cloned.1.call-done = bf16[2048,512]{1,0:T(8,128)(2,1)} async-done(((bf16[256,512]{1,0:T(8,128)(2,1)}), bf16[2048,512]{1,0:T(8,128)(2,1)}) %all-gather.17.cloned.1.call-update) | async-done | bytes 2097168 | tf_op jit(solution)/shard_map/all_gather | solution.py:142
  180.2 3.3 convolution_convert_fusion.7
  186.5 18.1 all-gather.1
  204.5 13.8 all-reduce.8.cloned.1.call-done
  218.3 1.7 multiply_reduce_fusion.2
  220.5 228.0 %all-gather.19.cloned.1.call-done = bf16[2048,4096]{1,0:T(8,128)(2,1)} async-done(((bf16[256,4096]{1,0:T(8,128)(2,1)}), bf16[2048,4096]{1,0:T(8,128)(2,1)}) %all-gather.19.cloned.1.call-update) | async-done | bytes 16777232 | tf_op jit(solution)/shard_map/all_gather | solution.py:161
  448.5 10.3 fusion.33
  458.8 217.8 %all-gather.21.cloned.1.call-done = bf16[2048,4096]{1,0:T(8,128)(2,1)} async-done(((bf16[256,4096]{1,0:T(8,128)(2,1)}), bf16[2048,4096]{1,0:T(8,128)(2,1)}) %all-gather.21.cloned.1.call-update) | async-done | bytes 16777232 | tf_op jit(solution)/shard_map/all_gather | solution.py:162
  676.7 10.2 fusion.34
  686.8 6.4 all-gather.25.cloned.1.call-done
  693.3 230.0 %all-gather.23.cloned.1.call-done = bf16[2048,4096]{1,0:T(8,128)(2,1)} async-done(((bf16[256,4096]{1,0:T(8,128)(2,1)}), bf16[2048,4096]{1,0:T(8,128)(2,1)}) %all-gather.23.cloned.1.call-update) | async-done | bytes 16777232 | tf_op jit(solution)/shard_map/all_gather | solution.py:168
  923.2 14.8 multiply_convert_fusion
  938.0 12.3 fusion.35
  950.3 12.5 fusion.7
  963.2 34.0 %all-reduce.10.cloned.1.call-done = bf16[256,2048]{1,0:T(8,128)(2,1)} async-done(((bf16[256,2048]{1,0:T(8,128)(2,1)}), bf16[256,2048]{1,0:T(8,128)(2,1)}) %all-reduce.10.cloned.1.call-update) | async-done | bytes 1048592 | tf_op jit(solution)/shard_map/psum | solution.py:189
  997.2 2.3 fusion.11
  999.5 4.0 fusion.12
  1010.3 1.7 convolution_convert_fusion.5
  1012.1 12.1 convolution_convert_fusion.6
  1024.3 2.2 convolution_convert_fusion.4
  1027.5 2.1 convolution_convert_fusion.2
  1029.6 22.1 %all-reduce.12.cloned.1.call-done = (bf16[256,512]{0,1:T(8,128)(2,1)}, bf16[256,2048]{1,0:T(8,128)(2,1)}) async-done(((bf16[256,512]{0,1:T(8,128)(2,1)}, bf16[256,2048]{1,0:T(8,128)(2,1)}), (bf16[256,512]{0,1:T(8,128)(2,1)}, bf16[256,2048]{1,0:T(8,128)(2,1)})) %all-reduce.12.cloned.1.call-update) | async-done | bytes 1310736 | tf_op jit(solution)/shard_map/psum | solution.py:202
  1051.7 3.2 convolution_convert_fusion.3
  1055.2 12.2 convolution_convert_fusion.1
  1067.5 12.2 convolution_convert_fusion
  1080.0 12.2 convert_bitcast_fusion
  1094.1 1.6 convert_element_type.141
  1096.4 3.8 multiply_reduce_fusion
  1100.2 37.3 %all-reduce.2 = (f32[2048]{0:T(1024)S(1)}, f32[2048]{0:T(1024)S(1)}) all-reduce(f32[2048]{0:T(1024)S(1)} %get-tuple-element.90, f32[2048]{0:T(1024)S(1)} %get-tuple-element.88), channel_id=3, replica_groups=mesh['dp'=8,'tensor'=4] {'dp'}, use_global_device_ids=true, to_apply=%region_15.16.clone | all-reduce | flops 4096 | bytes 32768
  1138.8 2.2 fusion.19
  1140.9 1.9 add_convert_fusion
  1142.8 8.2 reduce-scatter.10.cloned.1.call-done
  1151.0 1.8 convert_element_type.174
  1152.9 68.9 %reduce-scatter.14.cloned.1.call-done = bf16[256,512]{1,0:T(8,128)(2,1)} async-done(((bf16[2048,512]{1,0:T(8,128)(2,1)}), bf16[256,512]{1,0:T(8,128)(2,1)}) %reduce-scatter.14.cloned.1.call-update) | async-done | bytes 262160 | tf_op jit(solution)/shard_map/reduce_scatter | solution.py:221
  1221.7 1.8 convert_element_type.178
  1223.5 68.9 %reduce-scatter.12.cloned.1.call-done = bf16[256,512]{1,0:T(8,128)(2,1)} async-done(((bf16[2048,512]{1,0:T(8,128)(2,1)}), bf16[256,512]{1,0:T(8,128)(2,1)}) %reduce-scatter.12.cloned.1.call-update) | async-done | bytes 262160 | tf_op jit(solution)/shard_map/reduce_scatter | solution.py:221
  1292.4 1.8 convert_element_type.176
  1294.2 284.0 %reduce-scatter.16.cloned.1.call-done = bf16[256,4096]{1,0:T(8,128)(2,1)} async-done(((bf16[2048,4096]{1,0:T(8,128)(2,1)}), bf16[256,4096]{1,0:T(8,128)(2,1)}) %reduce-scatter.16.cloned.1.call-update) | async-done | bytes 2097168 | tf_op jit(solution)/shard_map/reduce_scatter | solution.py:221
  1578.2 4.1 convert_element_type.180
  1582.3 281.3 %reduce-scatter.18.cloned.1.call-done = bf16[256,4096]{1,0:T(8,128)(2,1)} async-done(((bf16[2048,4096]{1,0:T(8,128)(2,1)}), bf16[256,4096]{1,0:T(8,128)(2,1)}) %reduce-scatter.18.cloned.1.call-update) | async-done | bytes 2097168 | tf_op jit(solution)/shard_map/reduce_scatter | solution.py:221
  1863.6 4.1 convert_element_type.182
  1867.7 281.8 %reduce-scatter.20.cloned.1.call-done = bf16[256,4096]{0,1:T(8,128)(2,1)} async-done(((bf16[2048,4096]{0,1:T(8,128)(2,1)}), bf16[256,4096]{0,1:T(8,128)(2,1)}) %reduce-scatter.20.cloned.1.call-update) | async-done | bytes 2097168 | tf_op jit(solution)/shard_map/reduce_scatter | solution.py:221
  2149.5 4.3 copy.53
  (105 shorter events, 23.0 us)
Async XLA Ops:
  7.2 26.8 %all-gather.11.cloned.1.call-start = ((), (), s32[]{:S(2)}) async-start(), calls=%async_computation.7 | async-start | bytes 1310720 | tf_op jit(solution)/shard_map/all_gather | solution.py:133
  7.9 72.6 %all-gather.15.cloned.1.call-start = ((), (), s32[]{:S(2)}) async-start(), calls=%async_computation.9 | async-start | bytes 2359296 | tf_op jit(solution)/shard_map/all_gather | solution.py:140
  8.7 121.8 %all-gather.13.cloned.1.call-start = ((), (), s32[]{:S(2)}) async-start(), calls=%async_computation.8 | async-start | bytes 2359296 | tf_op jit(solution)/shard_map/all_gather | solution.py:141
  9.4 170.8 %all-gather.17.cloned.1.call-start = ((), (), s32[]{:S(2)}) async-start(), calls=%async_computation.10 | async-start | bytes 2359296 | tf_op jit(solution)/shard_map/all_gather | solution.py:142
  10.0 208.3 %all-reduce.8.cloned.1.call-start = ((), (), s32[]{:S(2)}) async-start(), calls=%async_computation.11 | async-start | bytes 2097152 | tf_op jit(solution)/shard_map/psum | solution.py:156
  80.5 49.9 %copy-start = (bf16[256,2048]{1,0:T(8,128)(2,1)S(1)}, bf16[256,2048]{1,0:T(8,128)(2,1)}, u32[]{:S(2)}) copy-start(bf16[256,2048]{1,0:T(8,128)(2,1)} %all-gather.11.cloned.1.call-done) | copy-start | bytes 3145732
  83.4 49.4 %copy-start.8 = (bf16[256,512]{0,1:T(8,128)(2,1)}, bf16[256,512]{0,1:T(8,128)(2,1)S(1)}, u32[]{:S(2)}) copy-start(bf16[256,512]{0,1:T(8,128)(2,1)S(1)} %copy.62) | copy-start | bytes 786436
  132.8 0.7 copy-start.13
  133.0 0.8 copy-start.4
  134.1 49.4 %copy-start.10 = (bf16[256,2,256]{2,0,1:T(8,128)(2,1)}, bf16[256,2,256]{2,0,1:T(8,128)(2,1)S(1)}, u32[]{:S(2)}) copy-start(bf16[256,2,256]{2,0,1:T(8,128)(2,1)S(1)} %convolution_convert_fusion.9) | copy-start | bytes 786436
  183.6 264.9 %all-gather.19.cloned.1.call-start = ((), (), s32[]{:S(2)}) async-start(), calls=%async_computation.12 | async-start | bytes 18874368 | tf_op jit(solution)/shard_map/all_gather | solution.py:161
  184.1 2.3 copy-start.16
  184.2 492.5 %all-gather.21.cloned.1.call-start = ((), (), s32[]{:S(2)}) async-start(), calls=%async_computation.13 | async-start | bytes 18874368 | tf_op jit(solution)/shard_map/all_gather | solution.py:162
  184.9 508.3 %all-gather.25.cloned.1.call-start = ((), (), s32[]{:S(2)}) async-start(), calls=%async_computation.16 | async-start | bytes 1310720 | tf_op jit(solution)/shard_map/all_gather | solution.py:134
  185.7 737.6 %all-gather.23.cloned.1.call-start = ((), (), s32[]{:S(2)}) async-start(), calls=%async_computation.14 | async-start | bytes 18874368 | tf_op jit(solution)/shard_map/all_gather | solution.py:168
  186.4 810.8 %all-reduce.10.cloned.1.call-start = ((), (), s32[]{:S(2)}) async-start(), calls=%async_computation.17 | async-start | bytes 2097152 | tf_op jit(solution)/shard_map/psum | solution.py:189
  218.3 1.7 copy-start.1
  220.5 456.1 %copy-start.2 = (bf16[256,2048]{1,0:T(8,128)(2,1)}, bf16[256,2048]{1,0:T(8,128)(2,1)S(1)}, u32[]{:S(2)}) copy-start(bf16[256,2048]{1,0:T(8,128)(2,1)S(1)} %multiply_convert_fusion.2) | copy-start | bytes 3145732
  962.7 89.0 %all-reduce.12.cloned.1.call-start = ((), (), s32[]{:S(2)}) async-start(), calls=%async_computation.24 | async-start | bytes 2621440 | tf_op jit(solution)/shard_map/psum | solution.py:202
  997.2 2.3 copy-start.6
  999.5 4.0 copy-start.3
  1006.0 3.0 copy-start.5
  1006.0 3.1 copy-start.9
  1006.0 3.3 copy-start.14
  1007.4 2.9 copy-start.7
  1012.1 128.8 %reduce-scatter.8.cloned.1.call-start = ((), (), s32[]{:S(2)}) async-start(), calls=%async_computation.15 | async-start | bytes 1310720 | tf_op jit(solution)/shard_map/reduce_scatter | solution.py:169
  1024.3 126.8 %reduce-scatter.10.cloned.1.call-start = ((), (), s32[]{:S(2)}) async-start(), calls=%async_computation.18 | async-start | bytes 2359296 | tf_op jit(solution)/shard_map/reduce_scatter | solution.py:221
  1026.5 1.0 copy-start.11
  1026.6 195.2 %reduce-scatter.14.cloned.1.call-start = ((), (), s32[]{:S(2)}) async-start(), calls=%async_computation.20 | async-start | bytes 2359296 | tf_op jit(solution)/shard_map/reduce_scatter | solution.py:221
  1029.6 262.8 %reduce-scatter.12.cloned.1.call-start = ((), (), s32[]{:S(2)}) async-start(), calls=%async_computation.19 | async-start | bytes 2359296 | tf_op jit(solution)/shard_map/reduce_scatter | solution.py:221
  1054.9 523.3 %reduce-scatter.16.cloned.1.call-start = ((), (), s32[]{:S(2)}) async-start(), calls=%async_computation.21 | async-start | bytes 18874368 | tf_op jit(solution)/shard_map/reduce_scatter | solution.py:221
  1067.4 796.1 %reduce-scatter.18.cloned.1.call-start = ((), (), s32[]{:S(2)}) async-start(), calls=%async_computation.22 | async-start | bytes 18874368 | tf_op jit(solution)/shard_map/reduce_scatter | solution.py:221
  1079.7 1069.8 %reduce-scatter.20.cloned.1.call-start = ((), (), s32[]{:S(2)}) async-start(), calls=%async_computation.23 | async-start | bytes 18874368 | tf_op jit(solution)/shard_map/reduce_scatter | solution.py:221
  1092.1 0.7 copy-start.17
  1092.2 3.5 copy-start.12
  1094.0 2.3 copy-start.15
Sparse Core Ops, SparseCore 0:
  9.6 19.4 all-gather.10
  31.2 49.2 all-gather.14
  82.6 47.7 all-gather.12
  132.4 47.7 all-gather.16
  183.7 34.5 all-reduce.7
  220.5 227.9 all-gather.18
  450.8 225.7 all-gather.20
  678.3 14.9 all-gather.24
  695.6 227.5 all-gather.22
  962.9 34.2 all-reduce.9
  1012.2 39.4 all-reduce.11
  1054.1 24.9 reduce-scatter.7
  1083.0 67.9 reduce-scatter.9
  1154.8 66.8 reduce-scatter.13
  1225.5 66.8 reduce-scatter.11
  1296.5 281.6 reduce-scatter.15
  1581.8 281.6 reduce-scatter.17
  1867.7 281.7 reduce-scatter.19
where the time goes:
time: 2170 us; the launch traced here: 2160 us
  waiting for transfers between devices  1890 us (87%)
  matrix products  135 us (6%)
  blocking collectives  77.6 us (4%)
  other arithmetic  31.2 us (1%)
    reduce_scatter x6, waiting for transfers between devices, body(): lax.psum_scatter(as_sent(ffn_terms + attn_terms), 'dp', scatter_dimension...  993 us
    all_gather x1, waiting for transfers between devices, body(): lax.all_gather(w_down, 'dp', axis=0, tiled=True)  230 us
    all_gather x1, waiting for transfers between devices, body(): lax.all_gather(w_gate, 'dp', axis=0, tiled=True)  228 us
    all_gather x1, waiting for transfers between devices, body(): lax.all_gather(w_up, 'dp', axis=0, tiled=True)  218 us
    all_gather x1, waiting for transfers between devices, body(): lax.all_gather(w_keyval, 'dp', axis=0, tiled=True)  47 us
    all_gather x1, waiting for transfers between devices, body(): lax.all_gather(w_out, 'dp', axis=0, tiled=True)  46.1 us
    dot_general x6, matrix products, mul_last(): lax.dot_general(left_mat, right_mat, (((1,), (1,)), ((), ())), preferred_...  45.7 us
    all_gather x1, waiting for transfers between devices, body(): lax.all_gather(w_query, 'dp', axis=0, tiled=True)  45 us
  transfers between devices with their start and end apart: 18, of which 16 were waited for; matrix products, arithmetic and copies ran while one was open for 5% of the time, Pallas kernels for 0%

commit v1 on v0

v1 whole, which is shorter than its diff:
```python
import functools

import jax
import jax.numpy as jnp
from jax import lax
from jax.experimental import pallas as pl
from jax.experimental.pallas import tpu as pltpu
from jax.sharding import PartitionSpec as P

HD = 256
WINDOW = 2048
NORM_EPS = 1e-06
MASKED = -1e30
BF16, F32 = jnp.bfloat16, jnp.float32
MESH = pl.DeviceIdType.MESH
ANY = pl.BlockSpec(memory_space=pl.ANY)
VMEM = pl.BlockSpec(memory_space=pltpu.VMEM)
SMEM = pl.BlockSpec(memory_space=pltpu.SMEM)
MIB = 1 << 20


def dot_nn(a, b):
    return lax.dot_general(a, b, (((1,), (0,)), ((), ())), preferred_element_type=F32)


def dot_nt(a, b):
    return lax.dot_general(a, b, (((1,), (1,)), ((), ())), preferred_element_type=F32)


def dot_tn(a, b):
    return lax.dot_general(a, b, (((0,), (0,)), ((), ())), preferred_element_type=F32)


class Net:
    def __init__(self, n, send, recv):
        self.n, self.nz = n, n // 2
        self.send, self.recv, self.used = send, recv, 0
        self.d = lax.axis_index("dp")
        self.t = lax.axis_index("tensor")
        self.z = self.d // 2
        self.x = self.d % 2
        self.dx = self.d + 1 - 2 * self.x
        self.ty = (self.t + 2) % 4
        self.tc = self.t + 1 - 2 * (self.t % 2)
        self.tcy = (self.tc + 2) % 4
        self.ends = []

    def take(self, count):
        first = self.used
        self.used += count
        return first

    def dp(self, other):
        return (other, self.t)

    def tensor(self, other):
        return (self.d, other)

    def make(self, src, dst, k, device):
        return pltpu.make_async_remote_copy(
            src_ref=src,
            dst_ref=dst,
            send_sem=self.send.at[k],
            recv_sem=self.recv.at[k],
            device_id=device,
            device_id_type=MESH,
        )

    def start(self, src, dst, k, device):
        self.make(src, dst, k, device).start()

    def landed(self, ref, k):
        self.make(ref, ref, k, self.tensor(self.tc)).wait_recv()

    def sent(self, ref, k):
        self.make(ref, ref, k, self.tensor(self.tc)).wait_send()

    def greet(self):
        barrier = pltpu.get_barrier_semaphore()

        @pl.loop(1, self.n)
        def _(m):
            pl.semaphore_signal(
                barrier, inc=1, device_id=self.dp((self.d + m) % self.n), device_id_type=MESH
            )

        for other in (self.ty, self.tc):
            pl.semaphore_signal(
                barrier, inc=1, device_id=self.tensor(other), device_id_type=MESH
            )
        pl.semaphore_wait(barrier, self.n + 1)

    def finish(self):
        for end in self.ends:
            end()


class TensorGather:
    def __init__(self, net, at):
        self.net, self.at, self.k = net, at, net.take(3)
        net.ends.append(self.end)

    def begin(self):
        net = self.net
        net.start(self.at(net.t), self.at(net.t), self.k, net.tensor(net.ty))
        net.start(self.at(net.t), self.at(net.t), self.k + 1, net.tensor(net.tc))

    def rest(self):
        net = self.net
        net.landed(self.at(net.ty), self.k)
        net.start(self.at(net.ty), self.at(net.ty), self.k + 2, net.tensor(net.tc))
        net.landed(self.at(net.tc), self.k + 1)
        net.landed(self.at(net.tcy), self.k + 2)

    def end(self):
        for i in range(3):
            self.net.sent(self.at(0), self.k + i)


class TensorScatter:
    def __init__(self, net, part, cl, yl):
        self.net, self.part, self.cl, self.yl, self.k = net, part, cl, yl, net.take(3)
        net.ends.append(self.end)

    def begin(self):
        net = self.net
        net.start(self.part.at[net.tcy], self.cl.at[1], self.k + 1, net.tensor(net.tc))
        net.start(self.part.at[net.tc], self.cl.at[0], self.k, net.tensor(net.tc))

    def rest(self):
        net = self.net
        net.landed(self.cl.at[1], self.k + 1)
        pair = self.part[net.ty].astype(F32) + self.cl[1].astype(F32)
        self.part[net.ty] = pair.astype(self.part.dtype)
        net.start(self.part.at[net.ty], self.yl, self.k + 2, net.tensor(net.ty))
        net.landed(self.cl.at[0], self.k)
        own = self.part[net.t].astype(F32) + self.cl[0].astype(F32)
        net.landed(self.yl, self.k + 2)
        return own + self.yl[...].astype(F32)

    def end(self):
        for i in range(3):
            self.net.sent(self.yl, self.k + i)


class Spread:
    def __init__(self, net, bufs, block, wide=False):
        self.net, self.bufs, self.block, self.wide = net, bufs, block, wide
        nz, n = net.nz, net.n
        self.zk = [net.take(2 * nz) for _ in bufs]
        self.xk = [net.take(nz) for _ in bufs]
        if wide:
            self.yk = [net.take(n) for _ in bufs]
            self.ck = [net.take(n) for _ in bufs]
        net.ends.append(self.end)

    def line(self, j, src, zb, right):
        net = self.net
        where = self.block(self.bufs[j], 2 * zb + net.x)
        if right:
            net.start(src, where, self.zk[j] + zb, net.dp(net.d + 2))
        else:
            net.start(src, where, self.zk[j] + net.nz + zb, net.dp(net.d - 2))

    def over_x(self, j, src, zb):
        net = self.net
        where = self.block(self.bufs[j], 2 * zb + net.x)
        net.start(src, where, self.xk[j] + zb, net.dp(net.dx))

    def over_y(self, j, src, idx):
        net = self.net
        net.start(src, self.bufs[j].at[1, idx], self.yk[j] + idx, net.tensor(net.ty))

    def begin(self, own=None):
        net = self.net
        own = own or [self.block(b, net.d) for b in self.bufs]
        for j, src in enumerate(own):

            @pl.when(net.z < net.nz - 1)
            def _():
                self.line(j, src, net.z, True)

            @pl.when(net.z > 0)
            def _():
                self.line(j, src, net.z, False)

            self.over_x(j, src, net.z)
            if self.wide:
                self.over_y(j, src, net.d)

    def hop(self, h):
        net = self.net
        nz = net.nz
        for j, buf in enumerate(self.bufs):

            @pl.when(net.z - h >= 0)
            def _():
                zb = net.z - h
                here = self.block(buf, 2 * zb + net.x)
                net.landed(here, self.zk[j] + zb)

                @pl.when(net.z < nz - 1)
                def _():
                    self.line(j, here, zb, True)

                self.over_x(j, here, zb)
                if self.wide:
                    self.over_y(j, here, 2 * zb + net.x)

            @pl.when(net.z + h <= nz - 1)
            def _():
                zb = net.z + h
                here = self.block(buf, 2 * zb + net.x)
                net.landed(here, self.zk[j] + nz + zb)

                @pl.when(net.z > 0)
                def _():
                    self.line(j, here, zb, False)

                self.over_x(j, here, zb)
                if self.wide:
                    self.over_y(j, here, 2 * zb + net.x)

    def hops(self):
        @pl.loop(1, self.net.nz)
        def _(h):
            self.hop(h)

    def cross(self):
        net = self.net

        @pl.loop(0, net.nz)
        def _(k):
            zb = (net.z + k) % net.nz
            idx = 2 * zb + 1 - net.x
            for j, buf in enumerate(self.bufs):
                net.landed(self.block(buf, idx), self.xk[j] + zb)
                if self.wide:
                    self.over_y(j, self.block(buf, idx), idx)

    def over(self):
        net = self.net

        @pl.loop(0, net.n)
        def _(k):
            idx = (2 * net.z + net.x + k) % net.n
            for j, buf in enumerate(self.bufs):
                net.landed(buf.at[1, idx], self.yk[j] + idx)
                net.start(
                    buf.at[pl.ds(0, 2), idx],
                    buf.at[pl.ds(2, 2), idx],
                    self.ck[j] + idx,
                    net.tensor(net.tc),
                )

    def done(self):
        net = self.net

        @pl.loop(0, net.n)
        def _(k):
            idx = (2 * net.z + net.x + k) % net.n
            for j, buf in enumerate(self.bufs):
                net.landed(buf.at[pl.ds(2, 2), idx], self.ck[j] + idx)

    def end(self):
        net = self.net

        @pl.loop(0, net.nz)
        def _(zb):
            for j, buf in enumerate(self.bufs):
                some = self.block(buf, 0)

                @pl.when((zb <= net.z) & (net.z < net.nz - 1))
                def _():
                    net.sent(some, self.zk[j] + zb)

                @pl.when((zb >= net.z) & (net.z > 0))
                def _():
                    net.sent(some, self.zk[j] + net.nz + zb)

                net.sent(some, self.xk[j] + zb)

        if self.wide:

            @pl.loop(0, net.n)
            def _(idx):
                for j, buf in enumerate(self.bufs):
                    net.sent(buf.at[0, 0], self.yk[j] + idx)
                    net.sent(buf.at[pl.ds(0, 2), 0], self.ck[j] + idx)


class Deal:
    def __init__(self, net, src, dst):
        self.net, self.src, self.dst, self.k = net, src, dst, net.take(net.n)
        net.ends.append(self.end)

    def begin(self):
        net = self.net

        @pl.loop(1, net.n)
        def _(m):
            to = (net.d + m) % net.n
            net.start(self.src(to), self.dst(net.d), self.k + m, net.dp(to))

    def done(self):
        net = self.net

        @pl.loop(1, net.n)
        def _(m):
            net.landed(self.dst((net.d - m + net.n) % net.n), self.k + m)

    def end(self):
        net = self.net

        @pl.loop(1, net.n)
        def _(m):
            net.sent(self.src(0), self.k + m)


class Scatter:
    def __init__(self, net, at, xl, rl, ll, mem):
        self.net, self.at, self.xl, self.rl, self.ll, self.mem = net, at, xl, rl, ll, mem
        self.xk, self.rk, self.lk = net.take(net.nz), net.take(net.nz), net.take(net.nz)
        net.ends.append(self.end)

    def order(self, k):
        nz = self.net.nz
        odd = k % 2
        return odd * (k // 2) + (1 - odd) * (nz - 1 - k // 2)

    def send_x(self, zb):
        net = self.net
        net.start(self.at(2 * zb + 1 - net.x), self.xl.at[zb], self.xk + zb, net.dp(net.dx))

    def begin(self):
        @pl.loop(0, self.net.nz)
        def _(k):
            self.send_x(self.order(k))

    def add(self, block, other):
        mem = self.mem
        mem.put(block, (mem.get(block).astype(F32) + mem.get(other).astype(F32)).astype(BF16))

    def meet(self, zb):
        net = self.net
        net.landed(self.xl.at[zb], self.xk + zb)
        self.add(self.at(2 * zb + net.x), self.xl.at[zb])

    def lines(self):
        net = self.net
        nz = net.nz

        @pl.loop(0, nz - 1)
        def _(k):
            far = nz - 1 - k

            @pl.when(far > net.z)
            def _():
                self.meet(far)
                here = self.at(2 * far + net.x)

                @pl.when(net.z > 0)
                def _():
                    net.landed(self.rl.at[far], self.rk + far)
                    self.add(here, self.rl.at[far])

                net.start(here, self.rl.at[far], self.rk + far, net.dp(net.d + 2))

            @pl.when(k < net.z)
            def _():
                self.meet(k)
                here = self.at(2 * k + net.x)

                @pl.when(net.z < nz - 1)
                def _():
                    net.landed(self.ll.at[k], self.lk + k)
                    self.add(here, self.ll.at[k])

                net.start(here, self.ll.at[k], self.lk + k, net.dp(net.d - 2))

        self.meet(net.z)

    def total(self, acc):
        net, mem = self.net, self.mem
        acc[...] = mem.get(self.at(2 * net.z + net.x)).astype(F32)

        @pl.when(net.z > 0)
        def _():
            net.landed(self.rl.at[net.z], self.rk + net.z)
            acc[...] += mem.get(self.rl.at[net.z]).astype(F32)

        @pl.when(net.z < net.nz - 1)
        def _():
            net.landed(self.ll.at[net.z], self.lk + net.z)
            acc[...] += mem.get(self.ll.at[net.z]).astype(F32)

    def end(self):
        net = self.net

        @pl.loop(0, net.nz)
        def _(zb):
            net.sent(self.xl.at[0], self.xk + zb)

            @pl.when(zb > net.z)
            def _():
                net.sent(self.rl.at[0], self.rk + zb)

            @pl.when(zb < net.z)
            def _():
                net.sent(self.ll.at[0], self.lk + zb)


class WideScatter:
    def __init__(self, net, part, own, cl, yl, xl, rl, ll, mem):
        self.net, self.part, self.own, self.cl, self.yl, self.mem = net, part, own, cl, yl, mem
        self.ck, self.yk = net.take(net.n), net.take(net.n)
        net.ends.append(self.end)
        self.inner = Scatter(net, lambda idx: own.at[0, idx], xl, rl, ll, mem)

    def order(self, k):
        net = self.net
        mine = k // net.nz
        zb = self.inner.order(k % net.nz)
        return 2 * zb + mine * net.x + (1 - mine) * (1 - net.x)

    def begin(self):
        net = self.net

        @pl.loop(0, net.n)
        def _(k):
            idx = self.order(k)
            net.start(
                self.part.at[pl.ds(2, 2), idx], self.cl.at[:, idx], self.ck + idx, net.tensor(net.tc)
            )

    def core(self):
        net = self.net

        @pl.loop(0, net.n)
        def _(k):
            idx = self.order(k)
            net.landed(self.cl.at[:, idx], self.ck + idx)
            self.inner.add(self.own.at[1, idx], self.cl.at[1, idx])
            net.start(self.own.at[1, idx], self.yl.at[idx], self.yk + idx, net.tensor(net.ty))
            self.inner.add(self.own.at[0, idx], self.cl.at[0, idx])

    def over(self):
        net = self.net

        @pl.loop(0, net.n)
        def _(k):
            idx = self.order(k)
            net.landed(self.yl.at[idx], self.yk + idx)
            self.inner.add(self.own.at[0, idx], self.yl.at[idx])

            @pl.when(k < net.nz)
            def _():
                self.inner.send_x(idx // 2)

    def end(self):
        net = self.net

        @pl.loop(0, net.n)
        def _(idx):
            net.sent(self.cl.at[:, 0], self.ck + idx)
            net.sent(self.yl.at[0], self.yk + idx)


class Direct:
    def get(self, ref):
        return ref[...]

    def put(self, ref, value):
        ref[...] = value


class Staged:
    def __init__(self, buf, sem):
        self.buf, self.sem = buf, sem

    def get(self, ref):
        copy = pltpu.make_async_copy(ref, self.buf, self.sem)
        copy.start()
        copy.wait()
        return self.buf[...]

    def put(self, ref, value):
        self.buf[...] = value
        copy = pltpu.make_async_copy(self.buf, ref, self.sem)
        copy.start()
        copy.wait()


def lane_row(gains, row, n):
    return jnp.concatenate([gains[8 * i + row : 8 * i + row + 1, :] for i in range(n)], axis=1)


def allowed_pairs(lens, rows):
    place_i = lax.broadcasted_iota(jnp.int32, (rows, 1), 0)
    place_j = lax.broadcasted_iota(jnp.int32, (1, rows), 1)
    segment_i = jnp.zeros((rows, 1), jnp.int32)
    segment_j = jnp.zeros((1, rows), jnp.int32)
    total = 0
    for k in range(lens.shape[1]):
        total = total + lens[0, k]
        segment_i += (place_i >= total).astype(jnp.int32)
        segment_j += (place_j >= total).astype(jnp.int32)
    distance = place_i - place_j
    return (segment_i == segment_j) & (distance >= 0) & (distance < WINDOW)


def softmax_head(query, key, allowed):
    scores = dot_nt(query, key) * HD ** (-0.5)
    scores = jnp.where(allowed, scores, MASKED)
    weights = jnp.exp(scores - jnp.max(scores, axis=-1, keepdims=True))
    return weights / jnp.sum(weights, axis=-1, keepdims=True)


def inverse_root(rows):
    return lax.rsqrt(jnp.mean(rows * rows, axis=-1, keepdims=True) + NORM_EPS)


def first_kernel(
    n, counts,
    lens, tok, go, gains, wq, wkv, wo, wg, wu, wd,
    wg_all, wu_all, wd_all, x_all, g_all, wq_out, wkv_out, wo_out, gains_out,
    query_out, keyval_out, context_out, normed_out, middle_out,
    send, recv, local, wq_all, wkv_all, wo_all, gains_all,
    group, kv_parts, branch, branch_c, branch_y, own_normed,
):
    net = Net(n, send, recv)
    d, t = net.d, net.t
    depth = wq.shape[0]
    quarter = wkv_all.shape[1]
    width = wg_all.shape[1]
    rows = tok.shape[0]

    def block(buf, idx):
        step = buf.shape[0] // n
        return buf.at[pl.ds(pl.multiple_of(idx * step, step), step)]

    def wide_block(buf, idx):
        return buf.at[0, idx]

    wkv_own = wkv.at[:, pl.ds(pl.multiple_of(t * quarter, 128), quarter)]
    tokens_g = TensorGather(net, lambda i: group.at[i])
    kv_g = TensorGather(net, lambda i: kv_parts.at[i])
    branch_s = TensorScatter(net, branch, branch_c, branch_y)
    first_w = Spread(net, [wq_all, wkv_all, gains_all], block)
    second_w = Spread(net, [wo_all], block)
    spread_g = Spread(net, [g_all], wide_block, wide=True)
    spread_x = Spread(net, [x_all], wide_block, wide=True)
    deals = [
        Deal(
            net,
            lambda to, w=w: w.at[:, pl.ds(pl.multiple_of(to * width, 128), width)],
            lambda frm, full=full: block(full, frm),
        )
        for w, full in ((wg, wg_all), (wu, wu_all), (wd, wd_all))
    ]
    assert net.used <= counts

    own_copies = [
        (tok, group.at[t]),
        (wq, block(wq_all, d)),
        (wkv_own, block(wkv_all, d)),
        (gains, block(gains_all, d)),
        (wo, block(wo_all, d)),
        (go, g_all.at[0, d]),
    ] + [(deal.src(d), deal.dst(d)) for deal in deals]
    own_copies = [
        pltpu.make_async_copy(a, b, local.at[i]) for i, (a, b) in enumerate(own_copies)
    ]
    for copy in own_copies:
        copy.start()
    net.greet()

    for copy in own_copies[:5]:
        copy.wait()
    tokens_g.begin()
    first_w.begin()
    second_w.begin()
    deals[0].begin()
    spread_g.begin([go])
    tokens_g.rest()

    @pl.loop(1, net.nz)
    def _(h):
        first_w.hop(h)
        second_w.hop(h)
        spread_g.hop(h)

    inputs = group[...].reshape(4 * rows, -1).astype(F32)
    root = inverse_root(inputs)
    first_w.cross()
    spread_g.cross()
    gain = lane_row(gains_all, 0, n)
    normed = (inputs * root * gain).astype(BF16)
    normed_out[...] = normed
    kv_parts[t] = dot_nn(normed, wkv_all[...]).astype(BF16)
    kv_g.begin()
    deals[1].begin()
    query_out[...] = dot_nn(normed, wq_all[...]).astype(BF16)
    kv_g.rest()
    for i in range(4):
        keyval_out[:, i * quarter : (i + 1) * quarter] = kv_parts[i]
    allowed = allowed_pairs(lens, 4 * rows)
    for h in range(query_out.shape[1] // HD):
        lanes = slice(h * HD, (h + 1) * HD)
        probs = softmax_head(query_out[:, lanes], keyval_out[:, :HD], allowed).astype(BF16)
        context_out[:, lanes] = dot_nn(probs, keyval_out[:, HD:]).astype(BF16)
    second_w.cross()
    branch[...] = dot_nt(context_out[...], wo_all[...]).astype(BF16).reshape(branch.shape)
    branch_s.begin()
    middle = tok_rows(group, t) + branch_s.rest()
    middle_out[...] = middle
    own_normed[...] = (middle * inverse_root(middle) * lane_row(gains_all, 1, n)).astype(BF16)
    own_x = pltpu.make_async_copy(own_normed, x_all.at[0, d], local.at[0])
    own_x.start()
    spread_x.begin([own_normed])
    deals[2].begin()
    outs = [
        pltpu.make_async_copy(a, b, local.at[1 + i])
        for i, (a, b) in enumerate(
            (
                (wq_all, wq_out),
                (wkv_all, wkv_out),
                (wo_all, wo_out),
                (gains_all, gains_out),
            )
        )
    ]
    for copy in outs:
        copy.start()
    own_copies[5].wait()
    spread_x.hops()
    spread_x.cross()
    spread_g.over()
    own_x.wait()
    spread_x.over()
    spread_g.done()
    spread_x.done()
    for deal in deals:
        deal.done()
    for copy in own_copies[6:] + outs:
        copy.wait()
    net.finish()


def tok_rows(group, t):
    return group[t].astype(F32)


def ffn_kernel(
    x_ref, g_ref, wg, wu, wd, o_ref, dx_ref, dwg_ref, dwu_ref, dwd_ref, acc_g, acc_u, acc_d
):
    step = pl.program_id(0)
    x, g = x_ref[...], g_ref[...]
    gate = dot_nn(x, wg[...])
    up = dot_nn(x, wu[...])
    grad_hidden = dot_nn(g, wd[...])
    root = (2.0 / jnp.pi) ** 0.5
    square = gate * gate
    tanh = jnp.tanh(root * gate * (1.0 + 0.044715 * square))
    half = 0.5 * (1.0 + tanh)
    gelu = gate * half
    slope = half + 0.5 * gate * (1.0 - tanh * tanh) * (root * (1.0 + 3 * 0.044715 * square))
    hidden = (gelu * up).astype(BF16)
    grad_gate = (grad_hidden * up * slope).astype(BF16)
    grad_up = (grad_hidden * gelu).astype(BF16)
    o_ref[...] = dot_nt(hidden, wd[...]).astype(BF16)
    dx_ref[...] = (dot_nt(grad_gate, wg[...]) + dot_nt(grad_up, wu[...])).astype(BF16)

    @pl.when(step == 0)
    def _():
        acc_g[...] = dot_tn(x, grad_gate)
        acc_u[...] = dot_tn(x, grad_up)
        acc_d[...] = dot_tn(g, hidden)

    @pl.when(step > 0)
    def _():
        acc_g[...] += dot_tn(x, grad_gate)
        acc_u[...] += dot_tn(x, grad_up)
        acc_d[...] += dot_tn(g, hidden)

    @pl.when(step == pl.num_programs(0) - 1)
    def _():
        dwg_ref[...] = acc_g[...].astype(BF16)
        dwu_ref[...] = acc_u[...].astype(BF16)
        dwd_ref[...] = acc_d[...].astype(BF16)


def second_kernel(
    n, counts, staged,
    lens, o_part, dx_part, dwg, dwu, dwd, tok, go, wq_all, wkv_all, wo_all, gains_all,
    query, keyval, context, normed, middle,
    block_out, grad_tokens, grad_gains, grad_wq, grad_wkv, grad_wo, grad_wg, grad_wu, grad_wd,
    dx_own, dx_c, dx_y, dx_x, dx_r, dx_l, o_own, o_c, o_y, o_x, o_r, o_l,
    send, recv, local, stage,
    acc, branch_rows, gkv, gkv_c, gkv_y, qpart, qpart_c, qpart_y,
    pq, pq_x, pq_r, pq_l, po, po_x, po_r, po_l, pk, pk_x, pk_r, pk_l, k_rows, acc_w, acc_k,
    gain_parts, gain_land, gain_sum, grad_query, own_grad,
):
    net = Net(n, send, recv)
    d, t = net.d, net.t
    depth = grad_wq.shape[0]
    width = dwg.shape[1]
    rows, features = tok.shape
    quarter = wkv_all.shape[1]

    def block(buf, idx):
        step = buf.shape[0] // n
        return buf.at[pl.ds(pl.multiple_of(idx * step, step), step)]

    mem = Staged(stage, local.at[0]) if staged else Direct()
    scatter_dx = WideScatter(net, dx_part, dx_own, dx_c, dx_y, dx_x, dx_r, dx_l, mem)
    scatter_o = WideScatter(net, o_part, o_own, o_c, o_y, o_x, o_r, o_l, mem)
    direct = Direct()
    scatter_q = Scatter(net, lambda i: block(pq, i), pq_x, pq_r, pq_l, direct)
    scatter_w = Scatter(net, lambda i: block(po, i), po_x, po_r, po_l, direct)
    scatter_k = Scatter(net, lambda i: block(pk, i), pk_x, pk_r, pk_l, direct)
    branch_g = TensorGather(net, lambda i: branch_rows.at[i])
    kv_s = TensorScatter(net, gkv, gkv_c, gkv_y)
    query_s = TensorScatter(net, qpart, qpart_c, qpart_y)
    kv_g = TensorGather(net, lambda i: k_rows.at[i])
    gain_deal = Deal(net, lambda to: gain_parts.at[to], lambda frm: gain_land.at[frm])
    gain_g = TensorGather(net, lambda i: gain_sum.at[i])
    deals = [
        Deal(
            net,
            lambda to, p=part: block(p, to),
            lambda frm, o=out: o.at[:, pl.ds(pl.multiple_of(frm * width, 128), width)],
        )
        for part, out in ((dwg, grad_wg), (dwu, grad_wu), (dwd, grad_wd))
    ]
    assert net.used <= counts
    copies = [(dx_part.at[pl.ds(0, 2)], dx_own), (o_part.at[pl.ds(0, 2)], o_own)] + [
        (deal.src(d), deal.dst(d)) for deal in deals
    ]
    copies = [pltpu.make_async_copy(a, b, local.at[1 + i]) for i, (a, b) in enumerate(copies)]
    for copy in copies:
        copy.start()
    net.greet()
    scatter_dx.begin()
    scatter_o.begin()
    copies[0].wait()
    scatter_dx.core()
    deals[0].begin()
    scatter_dx.over()
    copies[1].wait()
    scatter_o.core()
    scatter_dx.inner.lines()
    scatter_dx.inner.total(acc)

    rows_in = middle[...]
    root = inverse_root(rows_in)
    grad_normed = acc[...]
    gain = lane_row(gains_all, 1, n)
    scaled = grad_normed * gain
    inner = jnp.mean(scaled * rows_in, axis=-1, keepdims=True)
    grad_middle = go[...].astype(F32) + root * (scaled - rows_in * (root * root) * inner)
    own_grad[...] = grad_middle
    gain_ffn = jnp.sum(grad_normed * rows_in * root, axis=0, keepdims=True)
    branch_rows[t] = grad_middle.astype(BF16)
    branch_g.begin()
    deals[1].begin()
    scatter_o.over()
    branch_g.rest()
    grad_branch = branch_rows[...].reshape(4 * rows, features)
    grad_context = dot_nn(grad_branch, wo_all[...]).astype(BF16)
    chunk = 512
    for i in range(features // chunk):
        part = slice(i * chunk, (i + 1) * chunk)
        po[part, :] = dot_tn(grad_branch[:, part], context[...]).astype(BF16)
    scatter_w.begin()

    allowed = allowed_pairs(lens, 4 * rows)
    key, value = keyval[:, :HD], keyval[:, HD:]
    grad_key = jnp.zeros((4 * rows, HD), F32)
    grad_value = jnp.zeros((4 * rows, HD), F32)
    factor = HD ** (-0.5)
    for h in range(query.shape[1] // HD):
        lanes = slice(h * HD, (h + 1) * HD)
        probs = softmax_head(query[:, lanes], key, allowed)
        grad_head = grad_context[:, lanes]
        grad_probs = dot_nt(grad_head, value)
        inner = jnp.sum(grad_probs * probs, axis=-1, keepdims=True)
        grad_scores = (probs * (grad_probs - inner)).astype(BF16)
        grad_query[:, lanes] = (dot_nn(grad_scores, key) * factor).astype(BF16)
        grad_key += dot_tn(grad_scores, query[:, lanes]) * factor
        grad_value += dot_tn(probs.astype(BF16), grad_head)
    both = jnp.concatenate([grad_key, grad_value], axis=1).astype(BF16)
    for i in range(4):
        gkv[i] = both[:, i * quarter : (i + 1) * quarter]
    kv_s.begin()
    scatter_o.inner.lines()
    grad_kv = kv_s.rest().astype(BF16)
    term = dot_nt(grad_query[...], wq_all[...]) + dot_nt(grad_kv, wkv_all[...])
    qpart[...] = term.astype(BF16).reshape(qpart.shape)
    query_s.begin()
    for i in range(features // chunk):
        part = slice(i * chunk, (i + 1) * chunk)
        pq[part, :] = dot_tn(normed[:, part], grad_query[...]).astype(BF16)
        pk[part, :] = dot_tn(normed[:, part], grad_kv).astype(BF16)
    scatter_q.begin()
    scatter_k.begin()
    grad_normed = query_s.rest()

    rows_in = tok[...].astype(F32)
    root = inverse_root(rows_in)
    gain = lane_row(gains_all, 0, n)
    scaled = grad_normed * gain
    inner = jnp.mean(scaled * rows_in, axis=-1, keepdims=True)
    grad_tokens[...] = own_grad[...] + root * (scaled - rows_in * (root * root) * inner)
    gain_attn = jnp.sum(grad_normed * rows_in * root, axis=0, keepdims=True)
    for i in range(n):
        lanes = slice(i * depth, (i + 1) * depth)
        gain_parts[i, 0:1, :] = gain_attn[:, lanes]
        gain_parts[i, 1:2, :] = gain_ffn[:, lanes]
        gain_parts[i, 2:8, :] = jnp.zeros((6, depth), F32)
    gain_deal.begin()
    deals[2].begin()

    scatter_o.inner.total(acc)
    block_out[...] = (middle[...] + acc[...]).astype(BF16)
    scatter_w.lines()
    scatter_q.lines()
    scatter_k.lines()
    gain_land[d] = gain_parts[d]
    gain_deal.done()
    gain_sum[t] = jnp.sum(gain_land[...], axis=0)
    gain_g.begin()
    scatter_w.total(acc_w)
    grad_wo[...] = acc_w[...]
    scatter_q.total(acc_w)
    grad_wq[...] = acc_w[...]
    scatter_k.total(acc_k)
    k_rows[t] = acc_k[...]
    kv_g.begin()
    gain_g.rest()
    grad_gains[...] = jnp.sum(gain_sum[...], axis=0)
    kv_g.rest()
    for i in range(4):
        grad_wkv[:, i * quarter : (i + 1) * quarter] = k_rows[i]
    for deal in deals:
        deal.done()
    for copy in copies[2:]:
        copy.wait()
    net.finish()


def params(collective_id):
    return pltpu.CompilerParams(
        collective_id=collective_id, has_side_effects=True, vmem_limit_bytes=60 * MIB
    )


def body(
    n, tokens, grad_out, lengths, gain_attn, gain_ffn, w_query, w_keyval, w_out, w_gate, w_up, w_down
):
    nz = n // 2
    rows, features = tokens.shape
    depth, heads = w_query.shape
    quarter = w_keyval.shape[1] // 4
    width = w_gate.shape[1] // n
    group_rows = 4 * rows
    shape = jax.ShapeDtypeStruct
    gains = jnp.concatenate(
        [gain_attn[None], gain_ffn[None], jnp.zeros((6, depth), gain_attn.dtype)]
    ).astype(F32)

    counts = 9 + 4 * 3 * nz + 2 * (3 * nz + 2 * n) + 3 * n
    full = shape((features, width), BF16)
    wide = shape((4, n, rows, features), BF16)
    (
        wg_all, wu_all, wd_all, x_all, g_all, wq_all, wkv_all, wo_all, gains_all,
        query, keyval, context, normed, middle,
    ) = pl.pallas_call(
        functools.partial(first_kernel, n, counts),
        out_shape=(
            full, full, full, wide, wide,
            shape((features, heads), BF16),
            shape((features, quarter), BF16),
            shape((features, heads), BF16),
            shape((8 * n, depth), F32),
            shape((group_rows, heads), BF16),
            shape((group_rows, 2 * HD), BF16),
            shape((group_rows, heads), BF16),
            shape((group_rows, features), BF16),
            shape((rows, features), F32),
        ),
        in_specs=[SMEM] + [ANY] * 9,
        out_specs=(ANY,) * 9 + (VMEM,) * 5,
        scratch_shapes=[
            pltpu.SemaphoreType.DMA((counts,)),
            pltpu.SemaphoreType.DMA((counts,)),
            pltpu.SemaphoreType.DMA((9,)),
            pltpu.VMEM((features, heads), BF16),
            pltpu.VMEM((features, quarter), BF16),
            pltpu.VMEM((features, heads), BF16),
            pltpu.VMEM((8 * n, depth), F32),
            pltpu.VMEM((4, rows, features), BF16),
            pltpu.VMEM((4, group_rows, quarter), BF16),
            pltpu.VMEM((4, rows, features), BF16),
            pltpu.VMEM((2, rows, features), BF16),
            pltpu.VMEM((rows, features), BF16),
            pltpu.VMEM((rows, features), BF16),
        ],
        compiler_params=params(0),
        name="forward_attention",
    )(lengths, tokens, grad_out, gains, w_query, w_keyval, w_out, w_gate, w_up, w_down)

    all_rows = 4 * n * rows
    tile = 256
    row_tile = pl.BlockSpec((tile, features), lambda i: (i, 0))
    whole = pl.BlockSpec((features, width), lambda i: (0, 0), pipeline_mode=pl.Buffered(1))
    o_part, dx_part, dwg, dwu, dwd = pl.pallas_call(
        ffn_kernel,
        grid=(all_rows // tile,),
        out_shape=(
            shape((all_rows, features), BF16), shape((all_rows, features), BF16), full, full, full,
        ),
        in_specs=[row_tile, row_tile, whole, whole, whole],
        out_specs=(row_tile, row_tile, whole, whole, whole),
        scratch_shapes=[pltpu.VMEM((features, width), F32)] * 3,
        compiler_params=pltpu.CompilerParams(vmem_limit_bytes=60 * MIB),
        cost_estimate=pl.CostEstimate(
            flops=18 * all_rows * features * width,
            bytes_accessed=8 * all_rows * features,
            transcendentals=all_rows * width,
        ),
        name="feed_forward",
    )(
        x_all.reshape(all_rows, features), g_all.reshape(all_rows, features), wg_all, wu_all, wd_all
    )

    staged = n > 8
    counts = 2 * (2 * n + 3 * nz) + 3 * 3 * nz + 15 + n + 3 * n
    landing = [
        shape((2, n, rows, features), BF16),
        shape((2, n, rows, features), BF16),
        shape((n, rows, features), BF16),
        shape((nz, rows, features), BF16),
        shape((nz, rows, features), BF16),
        shape((nz, rows, features), BF16),
    ] * 2
    out_shape = [
        shape((rows, features), BF16),
        shape((rows, features), F32),
        shape((8, depth), F32),
        shape((depth, heads), F32),
        shape((depth, 4 * quarter), F32),
        shape((depth, heads), F32),
        shape((depth, n * width), BF16),
        shape((depth, n * width), BF16),
        shape((depth, n * width), BF16),
    ]
    out_specs = [VMEM] * 6 + [ANY] * 3
    in_vmem = []
    if staged:
        out_shape += landing
        out_specs += [ANY] * len(landing)
    else:
        in_vmem = [pltpu.VMEM(place.shape, place.dtype) for place in landing]

    def reduced(columns):
        return [pltpu.VMEM((features, columns), BF16)] + [
            pltpu.VMEM((nz, depth, columns), BF16)
        ] * 3

    results = pl.pallas_call(
        functools.partial(second_kernel, n, counts, staged),
        out_shape=tuple(out_shape),
        in_specs=[SMEM] + [ANY] * 5 + [VMEM] * 11,
        out_specs=tuple(out_specs),
        scratch_shapes=in_vmem
        + [
            pltpu.SemaphoreType.DMA((counts,)),
            pltpu.SemaphoreType.DMA((counts,)),
            pltpu.SemaphoreType.DMA((6,)),
            pltpu.VMEM((rows, features), BF16),
            pltpu.VMEM((rows, features), F32),
            pltpu.VMEM((4, rows, features), BF16),
            pltpu.VMEM((4, group_rows, quarter), BF16),
            pltpu.VMEM((2, group_rows, quarter), BF16),
            pltpu.VMEM((group_rows, quarter), BF16),
            pltpu.VMEM((4, rows, features), BF16),
            pltpu.VMEM((2, rows, features), BF16),
            pltpu.VMEM((rows, features), BF16),
        ]
        + reduced(heads)
        + reduced(heads)
        + reduced(quarter)
        + [
            pltpu.VMEM((4, depth, quarter), F32),
            pltpu.VMEM((depth, heads), F32),
            pltpu.VMEM((depth, quarter), F32),
            pltpu.VMEM((n, 8, depth), F32),
            pltpu.VMEM((n, 8, depth), F32),
            pltpu.VMEM((4, 8, depth), F32),
            pltpu.VMEM((group_rows, heads), BF16),
            pltpu.VMEM((rows, features), F32),
        ],
        compiler_params=params(1),
        name="backward_attention",
    )(
        lengths, o_part.reshape(4, n, rows, features), dx_part.reshape(4, n, rows, features),
        dwg, dwu, dwd, tokens, grad_out, wq_all, wkv_all, wo_all, gains_all,
        query, keyval, context, normed, middle,
    )
    block_out, grad_tokens, grad_gains, grad_wq, grad_wkv, grad_wo, grad_wg, grad_wu, grad_wd = (
        results[:9]
    )
    return (
        block_out,
        grad_tokens,
        grad_gains[0],
        grad_gains[1],
        grad_wq,
        grad_wkv,
        grad_wo,
        grad_wg.astype(F32),
        grad_wu.astype(F32),
        grad_wd.astype(F32),
    )


def solution(mesh):
    rows = P(("dp", "tensor"), None)
    both = P("dp", "tensor")
    return jax.shard_map(
        functools.partial(body, mesh.shape["dp"]),
        mesh=mesh,
        in_specs=(rows, rows, P("dp", None), P("dp"), P("dp"), both, P("dp", None), both, both, both, both),
        out_specs=(rows, rows, P("dp"), P("dp"), both, P("dp", None), both, both, both, both),
        check_vma=False,
    )
```

time: 2170 us -> 595 us (0.27)
  waiting for transfers between devices: 1890 us -> 0 us
  Pallas kernels: 0 us -> 577 us
  matrix products: 135 us -> 0 us
  blocking collectives: 77.6 us -> 0 us
    reduce_scatter x7 -> x0, waiting for transfers between devices: 993 us -> none  [the longest x6 993 us: body(): lax.psum_scatter(as_sent(ffn_terms + attn_terms), 'dp', scatter_dimension...]
    all_gather x8 -> x0, waiting for transfers between devices: 820 us -> none  [the longest x1 230 us: body(): lax.all_gather(w_down, 'dp', axis=0, tiled=True)]
    pallas_call x0 -> x3, Pallas kernels: none -> 577 us  [the longest x1 278 us: body(): pl.pallas_call(functools.partial(second_kernel, n, counts, staged), out_s...]
    dot_general x24 -> x0, matrix products: 135 us -> none  [the longest x6 45.7 us: mul_last(): lax.dot_general(left_mat, right_mat, (((1,), (1,)), ((), ())), preferred_...]
    psum x3 -> x0, waiting for transfers between devices: 69.8 us -> none  [the longest x1 34 us: body(): lax.psum(term.astype(jnp.bfloat16), 'tensor').astype(jnp.float32)]
    all_gather x2 -> x0, blocking collectives: 40.3 us -> none  [the longest x1 22.2 us: body(): lax.all_gather(gain_attn, 'dp', axis=0, tiled=True)]
    unnamed x1 -> x0, blocking collectives: 37.3 us -> none
  transfers between devices with their start and end apart: 18 -> 0, of which waited for: 16 -> 0; matrix products, arithmetic and copies ran while one was open for 5% -> 0% of each run, Pallas kernels for 0% -> 0%
where the time goes in v1:
time: 595 us; the launch traced here: 594 us
  Pallas kernels  577 us (97%)
  other arithmetic  9.92 us (2%)
  local copies, waits for them, and re-layouts  6.64 us (1%)
    pallas_call x1, Pallas kernels, body(): pl.pallas_call(functools.partial(second_kernel, n, counts, staged), out_s...  278 us
    pallas_call x1, Pallas kernels, body(): pl.pallas_call(functools.partial(first_kernel, n, counts), out_shape=(ful...  248 us
    pallas_call x1, Pallas kernels, body(): pl.pallas_call(ffn_kernel, grid=(all_rows // tile,), out_shape=(shape((al...  50.8 us

profile of v1, /device:TPU:0, one launch (start us, length us, event | category | flops | bytes accessed | tf_op | source)
XLA Modules:
  0.0 593.8 jit_solution(4286357323392862179)
XLA Ops:
  0.7 0.1 pad.2.clone
  0.7 0.7 broadcast_in_dim.9
  1.4 0.7 broadcast_in_dim.10
  2.0 0.7 maximum_convert_fusion.gains
  2.7 247.7 %forward_attention.1 = (bf16[2048,512]{1,0:T(8,128)(2,1)}, bf16[2048,512]{1,0:T(8,128)(2,1)}, bf16[2048,512]{1,0:T(8,128)(2,1)}, bf16[4,8,64,2048]{3,2,1,0:T(8,1...) custom-call(s32[1,3]{1,0:T(1,128)} %lens.3, ...), custom_call_target="tpu_custom_call" | custom-call | tf_op jit(solution)/shard_map/forward_attention/pallas_call | solution.py:878
  250.4 50.8 %feed_forward.1 = (bf16[2048,2048]{1,0:T(8,128)(2,1)}, bf16[2048,2048]{1,0:T(8,128)(2,1)}, bf16[2048,512]{1,0:T(8,128)(2,1)}, bf16[2048,512]{1,0:T(8,128)(2,1)}, bf16[2048,512]{1,0:T(8,128)(2,1)}) custom-call(bf16[2048,2048]{1,0:T(8,128)(2,1)} %bitcast.10, bf16[2048,2048]{1,0:T(8,128)(2,1)} %bitcast.11, bf16[2048,512]{1,0:T(8,128)(2,1)} %get-tuple-element.40.wg, ...), custom_call_target="tpu_custom_call" | custom-call | flops 38654705664 | bytes 33554432 | tf_op jit(solution)/shard_map/feed_forward/pallas_call | solution.py:917
  301.2 278.1 %backward_attention.1 = (bf16[64,2048]{1,0:T(8,128)(2,1)}, f32[64,2048]{1,0:T(8,128)}, f32[8,256]{1,0:T(8,128)}, f32[256,512]{1,0:T(8,128)}, f32[256,512]{1,0:T(...) custom-call(s32[1,3]{1,0:T(1,128)} %lens.3, ...), custom_call_target="tpu_custom_call" | custom-call | tf_op jit(solution)/shard_map/backward_attention/pallas_call | solution.py:971
  579.3 1.3 fusion
  580.6 0.0 copy-start.1
  580.6 4.2 convert_element_type.13
  584.9 0.0 copy-done.1
  584.9 0.0 copy-start
  584.9 2.5 convert_element_type.14
  587.4 0.0 copy-done
  587.4 0.0 copy-start.6
  587.4 0.0 copy-start.5
  587.4 0.0 copy-start.4
  587.4 2.5 convert_element_type.15
  589.9 0.0 copy-done.6
  589.9 0.0 copy-start.3
  589.9 0.0 copy-start.2
  589.9 0.7 copy.26
  590.6 0.0 copy-done.5
  590.6 0.8 copy.27
  591.4 0.0 copy-done.4
  591.4 0.8 copy.28
  592.2 0.0 copy-done.3
  592.2 0.8 copy.29
  593.0 0.0 copy-done.2
  593.0 0.8 copy.30
  (1 shorter events, 0.0 us)
Async XLA Ops:
  580.6 4.3 copy-start.1
  584.9 2.5 copy-start
  587.4 2.5 copy-start.6
  587.4 3.2 copy-start.5
  587.4 4.0 copy-start.4
  589.9 2.3 copy-start.3
  589.9 3.1 copy-start.2

commit v2 on v1

v2 whole, which is shorter than its diff:
```python
import functools

import jax
import jax.numpy as jnp
from jax import lax
from jax.experimental import pallas as pl
from jax.experimental.pallas import tpu as pltpu
from jax.sharding import PartitionSpec as P

HD = 256
WINDOW = 2048
NORM_EPS = 1e-06
MASKED = -1e30
BF16, F32 = jnp.bfloat16, jnp.float32
MESH = pl.DeviceIdType.MESH
ANY = pl.BlockSpec(memory_space=pl.ANY)
VMEM = pl.BlockSpec(memory_space=pltpu.VMEM)
SMEM = pl.BlockSpec(memory_space=pltpu.SMEM)
MIB = 1 << 20


def dot_nn(a, b):
    return lax.dot_general(a, b, (((1,), (0,)), ((), ())), preferred_element_type=F32)


def dot_nt(a, b):
    return lax.dot_general(a, b, (((1,), (1,)), ((), ())), preferred_element_type=F32)


def dot_tn(a, b):
    return lax.dot_general(a, b, (((0,), (0,)), ((), ())), preferred_element_type=F32)


class Net:
    def __init__(self, n, send, recv):
        self.n, self.nz = n, n // 2
        self.send, self.recv, self.used = send, recv, 0
        self.d = lax.axis_index("dp")
        self.t = lax.axis_index("tensor")
        self.z = self.d // 2
        self.x = self.d % 2
        self.dx = self.d + 1 - 2 * self.x
        self.ty = (self.t + 2) % 4
        self.tc = self.t + 1 - 2 * (self.t % 2)
        self.tcy = (self.tc + 2) % 4
        self.ends = []

    def take(self, count):
        first = self.used
        self.used += count
        return first

    def dp(self, other):
        return (other, self.t)

    def tensor(self, other):
        return (self.d, other)

    def make(self, src, dst, k, device):
        return pltpu.make_async_remote_copy(
            src_ref=src,
            dst_ref=dst,
            send_sem=self.send.at[k],
            recv_sem=self.recv.at[k],
            device_id=device,
            device_id_type=MESH,
        )

    def start(self, src, dst, k, device):
        self.make(src, dst, k, device).start()

    def landed(self, ref, k):
        self.make(ref, ref, k, self.tensor(self.tc)).wait_recv()

    def sent(self, ref, k):
        self.make(ref, ref, k, self.tensor(self.tc)).wait_send()

    def greet(self):
        barrier = pltpu.get_barrier_semaphore()

        @pl.loop(1, self.n)
        def _(m):
            pl.semaphore_signal(
                barrier, inc=1, device_id=self.dp((self.d + m) % self.n), device_id_type=MESH
            )

        for other in (self.ty, self.tc):
            pl.semaphore_signal(
                barrier, inc=1, device_id=self.tensor(other), device_id_type=MESH
            )
        pl.semaphore_wait(barrier, self.n + 1)

    def finish(self):
        for end in self.ends:
            end()


class TensorGather:
    def __init__(self, net, at):
        self.net, self.at, self.k = net, at, net.take(3)
        net.ends.append(self.end)

    def begin(self):
        net = self.net
        net.start(self.at(net.t), self.at(net.t), self.k, net.tensor(net.ty))
        net.start(self.at(net.t), self.at(net.t), self.k + 1, net.tensor(net.tc))

    def rest(self):
        net = self.net
        net.landed(self.at(net.ty), self.k)
        net.start(self.at(net.ty), self.at(net.ty), self.k + 2, net.tensor(net.tc))
        net.landed(self.at(net.tc), self.k + 1)
        net.landed(self.at(net.tcy), self.k + 2)

    def end(self):
        for i in range(3):
            self.net.sent(self.at(0), self.k + i)


class TensorScatter:
    def __init__(self, net, part, cl, yl):
        self.net, self.part, self.cl, self.yl, self.k = net, part, cl, yl, net.take(3)
        net.ends.append(self.end)

    def begin(self):
        net = self.net
        net.start(self.part.at[net.tcy], self.cl.at[1], self.k + 1, net.tensor(net.tc))
        net.start(self.part.at[net.tc], self.cl.at[0], self.k, net.tensor(net.tc))

    def rest(self):
        net = self.net
        net.landed(self.cl.at[1], self.k + 1)
        pair = self.part[net.ty].astype(F32) + self.cl[1].astype(F32)
        self.part[net.ty] = pair.astype(self.part.dtype)
        net.start(self.part.at[net.ty], self.yl, self.k + 2, net.tensor(net.ty))
        net.landed(self.cl.at[0], self.k)
        own = self.part[net.t].astype(F32) + self.cl[0].astype(F32)
        net.landed(self.yl, self.k + 2)
        return own + self.yl[...].astype(F32)

    def end(self):
        for i in range(3):
            self.net.sent(self.yl, self.k + i)


class Spread:
    def __init__(self, net, bufs, block):
        self.net, self.bufs, self.block = net, bufs, block
        self.zk = [net.take(2 * net.nz) for _ in bufs]
        self.xk = [net.take(net.nz) for _ in bufs]
        net.ends.append(self.end)

    def line(self, j, zb, right):
        net = self.net
        here = self.block(self.bufs[j], 2 * zb + net.x)
        if right:
            net.start(here, here, self.zk[j] + zb, net.dp(net.d + 2))
        else:
            net.start(here, here, self.zk[j] + net.nz + zb, net.dp(net.d - 2))

    def over_x(self, j, zb):
        net = self.net
        here = self.block(self.bufs[j], 2 * zb + net.x)
        net.start(here, here, self.xk[j] + zb, net.dp(net.dx))

    def begin(self):
        net = self.net
        for j in range(len(self.bufs)):

            @pl.when(net.z < net.nz - 1)
            def _():
                self.line(j, net.z, True)

            @pl.when(net.z > 0)
            def _():
                self.line(j, net.z, False)

            self.over_x(j, net.z)

    def hop(self, h):
        net = self.net
        nz = net.nz
        for j, buf in enumerate(self.bufs):

            @pl.when(net.z - h >= 0)
            def _():
                zb = net.z - h
                net.landed(self.block(buf, 2 * zb + net.x), self.zk[j] + zb)

                @pl.when(net.z < nz - 1)
                def _():
                    self.line(j, zb, True)

                self.over_x(j, zb)

            @pl.when(net.z + h <= nz - 1)
            def _():
                zb = net.z + h
                net.landed(self.block(buf, 2 * zb + net.x), self.zk[j] + nz + zb)

                @pl.when(net.z > 0)
                def _():
                    self.line(j, zb, False)

                self.over_x(j, zb)

    def cross(self):
        net = self.net

        @pl.loop(0, net.nz)
        def _(k):
            zb = (net.z + k) % net.nz
            for j, buf in enumerate(self.bufs):
                net.landed(self.block(buf, 2 * zb + 1 - net.x), self.xk[j] + zb)

    def end(self):
        net = self.net

        @pl.loop(0, net.nz)
        def _(zb):
            for j, buf in enumerate(self.bufs):
                some = self.block(buf, 0)

                @pl.when((zb <= net.z) & (net.z < net.nz - 1))
                def _():
                    net.sent(some, self.zk[j] + zb)

                @pl.when((zb >= net.z) & (net.z > 0))
                def _():
                    net.sent(some, self.zk[j] + net.nz + zb)

                net.sent(some, self.xk[j] + zb)


class WideSpread:
    def __init__(self, net, buf):
        self.net, self.buf = net, buf
        self.zk, self.xk = net.take(2 * net.nz), net.take(net.nz)
        self.yk, self.ck = net.take(2 * net.nz), net.take(4)
        net.ends.append(self.end)

    def onward(self, src, zb, right, left):
        net, buf = self.net, self.buf
        if right:

            @pl.when(net.z < net.nz - 1)
            def _():
                net.start(src, buf.at[0, zb], self.zk + zb, net.dp(net.d + 2))

        if left:

            @pl.when(net.z > 0)
            def _():
                net.start(src, buf.at[0, zb], self.zk + net.nz + zb, net.dp(net.d - 2))

        net.start(src, buf.at[2, zb], self.yk + zb, net.tensor(net.ty))
        net.start(src, buf.at[1, zb], self.xk + zb, net.dp(net.dx))

    def begin(self, own):
        self.onward(own, self.net.z, True, True)

    def hop(self, h):
        net, buf = self.net, self.buf

        @pl.when(net.z - h >= 0)
        def _():
            zb = net.z - h
            net.landed(buf.at[0, zb], self.zk + zb)
            self.onward(buf.at[0, zb], zb, True, False)

        @pl.when(net.z + h <= net.nz - 1)
        def _():
            zb = net.z + h
            net.landed(buf.at[0, zb], self.zk + net.nz + zb)
            self.onward(buf.at[0, zb], zb, False, True)

    def hops(self):
        @pl.loop(1, self.net.nz)
        def _(h):
            self.hop(h)

    def cross(self):
        net, buf = self.net, self.buf

        @pl.loop(0, net.nz)
        def _(k):
            zb = (net.z + k) % net.nz
            net.landed(buf.at[1, zb], self.xk + zb)
            net.start(buf.at[1, zb], buf.at[3, zb], self.yk + net.nz + zb, net.tensor(net.ty))

    def over(self, x):
        net = self.net

        @pl.loop(0, net.nz)
        def _(k):
            zb = (net.z + k) % net.nz
            net.landed(self.buf.at[2 + x, zb], self.yk + x * net.nz + zb)

    def core(self, slot):
        net = self.net
        net.start(self.buf.at[slot], self.buf.at[4 + slot], self.ck + slot, net.tensor(net.tc))

    def core_done(self, slot):
        self.net.landed(self.buf.at[4 + slot], self.ck + slot)

    def end(self):
        net = self.net
        some = self.buf.at[0, 0]

        @pl.loop(0, net.nz)
        def _(zb):
            @pl.when((zb <= net.z) & (net.z < net.nz - 1))
            def _():
                net.sent(some, self.zk + zb)

            @pl.when((zb >= net.z) & (net.z > 0))
            def _():
                net.sent(some, self.zk + net.nz + zb)

            net.sent(some, self.xk + zb)
            net.sent(some, self.yk + zb)
            net.sent(some, self.yk + net.nz + zb)

        for slot in range(4):
            net.sent(self.buf.at[0], self.ck + slot)


class Deal:
    def __init__(self, net, src, dst):
        self.net, self.src, self.dst, self.k = net, src, dst, net.take(net.n)
        net.ends.append(self.end)

    def send(self, m):
        net = self.net
        to = (net.d + m) % net.n
        net.start(self.src(to), self.dst(net.d), self.k + m, net.dp(to))

    def begin(self):
        pl.loop(1, self.net.n)(self.send)

    def done(self):
        net = self.net

        @pl.loop(1, net.n)
        def _(m):
            net.landed(self.dst((net.d - m + net.n) % net.n), self.k + m)

    def end(self):
        net = self.net

        @pl.loop(1, net.n)
        def _(m):
            net.sent(self.src(0), self.k + m)


class Flow:
    def __init__(self, deals):
        self.todo = [(deal, m) for deal in deals for m in range(1, deal.net.n)]
        self.total, self.gone, self.share = len(self.todo), 0, 0.0

    def pump(self, share):
        self.share += share
        upto = min(self.total, round(self.share * self.total))
        for deal, m in self.todo[self.gone : upto]:
            deal.send(m)
        self.gone = max(upto, self.gone)

    def rest(self):
        self.pump(1.0)


class Scatter:
    def __init__(self, net, own, other, xl, zl, mem):
        self.net, self.own, self.other, self.xl, self.zl, self.mem = net, own, other, xl, zl, mem
        self.xk, self.rk, self.lk = net.take(net.nz), net.take(net.nz), net.take(net.nz)
        net.ends.append(self.end)

    def order(self, k):
        odd = k % 2
        return odd * (k // 2) + (1 - odd) * (self.net.nz - 1 - k // 2)

    def send_x(self, zb):
        net = self.net
        net.start(self.other(zb), self.xl.at[zb], self.xk + zb, net.dp(net.dx))

    def begin(self):
        @pl.loop(0, self.net.nz)
        def _(k):
            self.send_x(self.order(k))

    def add(self, block, other):
        mem = self.mem
        mem.put(block, (mem.get(block).astype(F32) + mem.get(other).astype(F32)).astype(BF16))

    def meet(self, zb):
        net = self.net
        net.landed(self.xl.at[zb], self.xk + zb)
        self.add(self.own(zb), self.xl.at[zb])

    def lines(self):
        net = self.net
        nz = net.nz

        @pl.loop(0, nz - 1)
        def _(k):
            far = nz - 1 - k

            @pl.when(far > net.z)
            def _():
                self.meet(far)
                here = self.own(far)

                @pl.when(net.z > 0)
                def _():
                    net.landed(self.zl.at[far], self.rk + far)
                    self.add(here, self.zl.at[far])

                net.start(here, self.zl.at[far], self.rk + far, net.dp(net.d + 2))

            @pl.when(k < net.z)
            def _():
                self.meet(k)
                here = self.own(k)

                @pl.when(net.z < nz - 1)
                def _():
                    net.landed(self.zl.at[k], self.lk + k)
                    self.add(here, self.zl.at[k])

                last = (k == net.z - 1).astype(jnp.int32)
                net.start(
                    here, self.zl.at[last * nz + (1 - last) * k], self.lk + k, net.dp(net.d - 2)
                )

        self.meet(net.z)

    def total(self, acc):
        net, mem = self.net, self.mem
        acc[...] = mem.get(self.own(net.z)).astype(F32)

        @pl.when(net.z > 0)
        def _():
            net.landed(self.zl.at[net.z], self.rk + net.z)
            acc[...] += mem.get(self.zl.at[net.z]).astype(F32)

        @pl.when(net.z < net.nz - 1)
        def _():
            net.landed(self.zl.at[net.nz], self.lk + net.z)
            acc[...] += mem.get(self.zl.at[net.nz]).astype(F32)

    def end(self):
        net = self.net

        @pl.loop(0, net.nz)
        def _(zb):
            net.sent(self.xl.at[0], self.xk + zb)

            @pl.when(zb > net.z)
            def _():
                net.sent(self.zl.at[0], self.rk + zb)

            @pl.when(zb < net.z)
            def _():
                net.sent(self.zl.at[0], self.lk + zb)


class WideScatter(Scatter):
    def __init__(self, net, cl, yl, xl, zl, mem, tiles):
        self.cl, self.yl, self.tiles = cl, yl, tiles
        self.ck, self.yk = net.take(4 * tiles), net.take(2 * net.nz)
        super().__init__(net, lambda zb: cl.at[0, zb], lambda zb: cl.at[1, zb], xl, zl, mem)
        net.ends.append(self.wide_end)

    def place(self, yx, sub):
        blocks = self.net.nz // self.tiles
        return self.cl.at[yx, pl.ds(sub * blocks, blocks)]

    def to_core(self, stage, yx, sub):
        net = self.net
        net.start(stage, self.place(yx, sub), self.ck + yx * self.tiles + sub, net.tensor(net.tc))

    def core_sent(self, yx, sub):
        self.net.sent(self.place(0, 0), self.ck + yx * self.tiles + sub)

    def keep(self, value, yx, sub):
        place = self.place(yx, sub)
        self.net.landed(place, self.ck + yx * self.tiles + sub)
        value = value.reshape(place.shape) + self.mem.get(place).astype(F32)
        self.mem.put(place, value.astype(BF16))

    def to_y(self, x, zb):
        net = self.net
        net.start(
            self.cl.at[2 + x, zb], self.yl.at[x, zb], self.yk + x * net.nz + zb, net.tensor(net.ty)
        )

    def all_to_y(self, x):
        @pl.loop(0, self.net.nz)
        def _(k):
            self.to_y(x, self.order(k))

    def from_y(self, x, zb):
        net = self.net
        net.landed(self.yl.at[x, zb], self.yk + x * net.nz + zb)
        self.add(self.cl.at[x, zb], self.yl.at[x, zb])

    def over(self):
        @pl.loop(0, self.net.nz)
        def _(k):
            zb = self.order(k)
            self.from_y(1, zb)
            self.send_x(zb)

    def meet(self, zb):
        self.from_y(0, zb)
        super().meet(zb)

    def wide_end(self):
        net = self.net

        @pl.loop(0, net.nz)
        def _(zb):
            net.sent(self.yl.at[0, 0], self.yk + zb)
            net.sent(self.yl.at[0, 0], self.yk + net.nz + zb)


class Direct:
    def get(self, ref):
        return ref[...]

    def put(self, ref, value):
        ref[...] = value


class Staged:
    def __init__(self, buf, sem):
        self.buf, self.sem = buf, sem

    def view(self, ref):
        return self.buf if len(ref.shape) == 3 else self.buf.at[0]

    def get(self, ref):
        view = self.view(ref)
        copy = pltpu.make_async_copy(ref, view, self.sem)
        copy.start()
        copy.wait()
        return view[...]

    def put(self, ref, value):
        view = self.view(ref)
        view[...] = value
        copy = pltpu.make_async_copy(view, ref, self.sem)
        copy.start()
        copy.wait()


def lane_row(gains, row, n):
    return jnp.concatenate([gains[8 * i + row : 8 * i + row + 1, :] for i in range(n)], axis=1)


def allowed_pairs(lens, rows):
    place_i = lax.broadcasted_iota(jnp.int32, (rows, 1), 0)
    place_j = lax.broadcasted_iota(jnp.int32, (1, rows), 1)
    segment_i = jnp.zeros((rows, 1), jnp.int32)
    segment_j = jnp.zeros((1, rows), jnp.int32)
    total = 0
    for k in range(lens.shape[1]):
        total = total + lens[0, k]
        segment_i += (place_i >= total).astype(jnp.int32)
        segment_j += (place_j >= total).astype(jnp.int32)
    distance = place_i - place_j
    return (segment_i == segment_j) & (distance >= 0) & (distance < WINDOW)


def softmax_head(query, key, allowed):
    scores = dot_nt(query, key) * HD ** (-0.5)
    scores = jnp.where(allowed, scores, MASKED)
    weights = jnp.exp(scores - jnp.max(scores, axis=-1, keepdims=True))
    return weights / jnp.sum(weights, axis=-1, keepdims=True)


def inverse_root(rows):
    return lax.rsqrt(jnp.mean(rows * rows, axis=-1, keepdims=True) + NORM_EPS)


def feed_forward(x, g, wg, wu, wd):
    gate = dot_nn(x, wg)
    up = dot_nn(x, wu)
    grad_hidden = dot_nn(g, wd)
    root = (2.0 / jnp.pi) ** 0.5
    square = gate * gate
    tanh = jnp.tanh(root * gate * (1.0 + 0.044715 * square))
    half = 0.5 * (1.0 + tanh)
    gelu = gate * half
    slope = half + 0.5 * gate * (1.0 - tanh * tanh) * (root * (1.0 + 3 * 0.044715 * square))
    hidden = (gelu * up).astype(BF16)
    grad_gate = (grad_hidden * up * slope).astype(BF16)
    grad_up = (grad_hidden * gelu).astype(BF16)
    return hidden, grad_gate, grad_up


def row_block(n, buf, idx):
    step = buf.shape[0] // n
    return buf.at[pl.ds(pl.multiple_of(idx * step, step), step)]


def lanes_at(start, size):
    return pl.ds(pl.multiple_of(start, 128), size)


def first_kernel(
    n, counts, pumps,
    lens, tok, go, gains, wq, wkv, wo, wg, wu, wd,
    wg_all, wu_all, wd_all, x_all, g_all, wq_out, wkv_out, wo_out, gains_out,
    query_out, keyval_out, context_out, normed_out, middle_out, acts_out, dwg_out, dwu_out, dwd_out,
    send, recv, local, wq_all, wkv_all, wo_all, gains_all,
    group, kv_parts, branch, branch_c, branch_y, own_normed,
    w_part, x_tile, g_tile, acc_g, acc_u, acc_d,
):
    net = Net(n, send, recv)
    d, t = net.d, net.t
    quarter = wkv_all.shape[1]
    width = wg_all.shape[1]
    cut = acts_out.shape[2]
    rows, features = tok.shape

    def block(buf, idx):
        return row_block(n, buf, idx)

    wkv_own = wkv.at[:, lanes_at(t * quarter, quarter)]
    tokens_g = TensorGather(net, lambda i: group.at[i])
    kv_g = TensorGather(net, lambda i: kv_parts.at[i])
    branch_s = TensorScatter(net, branch, branch_c, branch_y)
    first_w = Spread(net, [wq_all, wkv_all, gains_all], block)
    second_w = Spread(net, [wo_all], block)
    spread_g = WideSpread(net, g_all)
    spread_x = WideSpread(net, x_all)
    deals = [
        Deal(
            net,
            lambda to, w=w, at=at: w.at[:, lanes_at(to * width + at, cut)],
            lambda frm, full=full, at=at: block(full, frm).at[:, pl.ds(at, cut)],
        )
        for at in range(0, width, cut)
        for w, full in ((wg, wg_all), (wu, wu_all), (wd, wd_all))
    ]
    assert net.used <= counts
    flow = Flow(deals)

    own_copies = [
        (tok, group.at[t]),
        (wq, block(wq_all, d)),
        (wkv_own, block(wkv_all, d)),
        (gains, block(gains_all, d)),
        (wo, block(wo_all, d)),
        (go, g_all.at[0, net.z]),
    ] + [
        (w.at[:, lanes_at(d * width, width)], block(full, d))
        for w, full in ((wg, wg_all), (wu, wu_all), (wd, wd_all))
    ]
    own_copies = [
        pltpu.make_async_copy(a, b, local.at[i]) for i, (a, b) in enumerate(own_copies)
    ]
    for copy in own_copies:
        copy.start()
    net.greet()

    for copy in own_copies[:4]:
        copy.wait()
    tokens_g.begin()
    first_w.begin()
    flow.pump(pumps[0])
    own_copies[4].wait()
    tokens_g.rest()
    second_w.begin()

    @pl.loop(1, net.nz)
    def _(h):
        first_w.hop(h)

        @pl.when(h > 1)
        def _():
            second_w.hop(h - 1)

    flow.pump(pumps[1])
    inputs = group[...].reshape(4 * rows, features).astype(F32)
    root = inverse_root(inputs)
    first_w.cross()
    second_w.hop(net.nz - 1)
    spread_g.begin(go)
    flow.pump(pumps[2])
    gain = lane_row(gains_all, 0, n)
    normed = (inputs * root * gain).astype(BF16)
    normed_out[...] = normed
    kv_parts[t] = dot_nn(normed, wkv_all[...]).astype(BF16)
    kv_g.begin()
    query_out[...] = dot_nn(normed, wq_all[...]).astype(BF16)
    spread_g.hop(1)
    kv_g.rest()
    for i in range(4):
        keyval_out[:, i * quarter : (i + 1) * quarter] = kv_parts[i]
    allowed = allowed_pairs(lens, 4 * rows)
    flow.pump(pumps[3])
    for h in range(query_out.shape[1] // HD):
        lanes = slice(h * HD, (h + 1) * HD)
        probs = softmax_head(query_out[:, lanes], keyval_out[:, :HD], allowed).astype(BF16)
        context_out[:, lanes] = dot_nn(probs, keyval_out[:, HD:]).astype(BF16)
    pl.loop(2, net.nz)(spread_g.hop)
    second_w.cross()
    branch[...] = dot_nt(context_out[...], wo_all[...]).astype(BF16).reshape(branch.shape)
    branch_s.begin()
    flow.pump(pumps[4])
    spread_g.cross()
    middle = group[t].astype(F32) + branch_s.rest()
    middle_out[...] = middle
    own_normed[...] = (middle * inverse_root(middle) * lane_row(gains_all, 1, n)).astype(BF16)
    own_x = pltpu.make_async_copy(own_normed, x_all.at[0, net.z], local.at[0])
    own_x.start()
    spread_x.begin(own_normed)
    flow.pump(pumps[5])
    outs = [
        pltpu.make_async_copy(a, b, local.at[1 + i])
        for i, (a, b) in enumerate(
            (
                (wq_all, wq_out),
                (wkv_all, wkv_out),
                (wo_all, wo_out),
                (gains_all, gains_out),
            )
        )
    ]
    for copy in outs:
        copy.start()
    own_copies[5].wait()
    own_x.wait()
    spread_x.hops()
    flow.pump(pumps[6])
    spread_x.core(0)
    spread_g.core(0)
    spread_x.cross()
    flow.pump(pumps[7])
    spread_x.core(1)
    spread_g.core(1)
    for x in range(2):
        spread_g.over(x)
        spread_g.core(2 + x)
    flow.pump(pumps[8])
    for slot in range(4):
        spread_g.core_done(slot)

    for i, (copy, deal, full) in enumerate(
        zip(own_copies[6:], deals[:3], (wg_all, wu_all, wd_all))
    ):
        copy.wait()
        deal.done()
        pltpu.make_async_copy(full.at[:, pl.ds(0, cut)], w_part.at[i], local.at[5 + i]).start()
    for acc in (acc_g, acc_u, acc_d):
        acc[...] = jnp.zeros_like(acc)
    for i, full in enumerate((wg_all, wu_all, wd_all)):
        pltpu.make_async_copy(full.at[:, pl.ds(0, cut)], w_part.at[i], local.at[5 + i]).wait()
    flow.pump(pumps[9])
    tile_blocks = x_tile.shape[0]
    tile = tile_blocks * rows

    @pl.loop(0, 8)
    def _(k):
        slot = k % 2 + 4 * ((k // 2) % 2) + 2 * (k // 4)
        for at, slot_from in ((2, 0), (3, 1), (6, 2), (7, 3)):

            @pl.when(k == at)
            def _():
                spread_x.core_done(slot_from)

        for at, x in ((4, 0), (5, 1)):

            @pl.when(k == at)
            def _():
                spread_x.over(x)
                spread_x.core(2 + x)

        @pl.loop(0, net.nz // tile_blocks)
        def _(sub):
            part = pl.ds(sub * tile_blocks, tile_blocks)
            loads = [
                pltpu.make_async_copy(a.at[slot, part], b, local.at[5 + i])
                for i, (a, b) in enumerate(((x_all, x_tile), (g_all, g_tile)))
            ]
            for load in loads:
                load.start()
            for load in loads:
                load.wait()
            x = x_tile[...].reshape(tile, features)
            g = g_tile[...].reshape(tile, features)
            hidden, grad_gate, grad_up = feed_forward(x, g, w_part[0], w_part[1], w_part[2])
            start = pl.multiple_of((slot * net.nz + sub * tile_blocks) * rows, tile)
            acts_out[0, pl.ds(start, tile), :] = hidden
            acts_out[1, pl.ds(start, tile), :] = grad_gate
            acts_out[2, pl.ds(start, tile), :] = grad_up
            acc_g[...] += dot_tn(x, grad_gate)
            acc_u[...] += dot_tn(x, grad_up)
            acc_d[...] += dot_tn(g, hidden)

    dwg_out[...] = acc_g[...].astype(BF16)
    dwu_out[...] = acc_u[...].astype(BF16)
    dwd_out[...] = acc_d[...].astype(BF16)
    flow.rest()
    for deal in deals[3:]:
        deal.done()
    for copy in outs:
        copy.wait()
    net.finish()


def second_kernel(
    n, counts, staged, pumps,
    lens, x_all, g_all, acts, wg_all, wu_all, wd_all, dwg, dwu, dwd,
    wq_all, wkv_all, wo_all, normed,
    tok, go, gains_all, query, keyval, context, middle,
    block_out, grad_tokens, grad_gains, grad_wq, grad_wkv, grad_wo, grad_wg, grad_wu, grad_wd,
    dx_c, dx_y, dx_x, dx_z, o_c, o_y, o_x, o_z,
    send, recv, local, stage, dw_part,
    acc, branch_rows, gkv, gkv_c, gkv_y, qpart, qpart_c, qpart_y,
    pq_x, pq_z, po_x, po_z, pk_x, pk_z, k_rows, acc_w, acc_k,
    gain_parts, gain_land, gain_sum, grad_query, own_grad,
):
    net = Net(n, send, recv)
    d, t = net.d, net.t
    nz = net.nz
    depth, heads = grad_wq.shape
    features, width = wg_all.shape
    cut = acts.shape[2]
    two = cut < width
    rows = tok.shape[0]
    quarter = wkv_all.shape[1]
    blocks = 256 // rows
    tile = blocks * rows
    subs = nz // blocks

    def block(buf, idx):
        return row_block(n, buf, idx)

    def own_of(buf):
        return lambda zb: block(buf, 2 * zb + net.x)

    def other_of(buf):
        return lambda zb: block(buf, 2 * zb + 1 - net.x)

    mem = Staged(stage, local.at[0]) if staged else Direct()
    scatter_dx = WideScatter(net, dx_c, dx_y, dx_x, dx_z, mem, subs)
    scatter_o = WideScatter(net, o_c, o_y, o_x, o_z, mem, subs)
    branch_g = TensorGather(net, lambda i: branch_rows.at[i])
    kv_s = TensorScatter(net, gkv, gkv_c, gkv_y)
    query_s = TensorScatter(net, qpart, qpart_c, qpart_y)
    kv_g = TensorGather(net, lambda i: k_rows.at[i])
    gain_deal = Deal(net, lambda to: gain_parts.at[to], lambda frm: gain_land.at[frm])
    gain_g = TensorGather(net, lambda i: gain_sum.at[i])
    outs = (grad_wg, grad_wu, grad_wd)
    deals = [
        Deal(
            net,
            lambda to, p=part: block(p, to),
            lambda frm, o=out: o.at[:, lanes_at(frm * width, cut)],
        )
        for part, out in zip((dwg, dwu, dwd), outs)
    ]
    if two:
        deals += [
            Deal(
                net,
                lambda to, i=i: block(dw_part.at[i], to),
                lambda frm, o=out: o.at[:, lanes_at(frm * width + cut, cut)],
            )
            for i, out in enumerate(outs)
        ]
    flow = Flow(deals[:3])
    late = Flow(deals[3:])
    copies = [
        pltpu.make_async_copy(deal.src(d), deal.dst(d), local.at[1 + i])
        for i, deal in enumerate(deals)
    ]
    for copy in copies[:3]:
        copy.start()
    net.greet()
    flow.pump(pumps[0])

    def ffn(wg_v, wu_v, wd_v, acc_g, acc_u, acc_d, x_tiles, g_tiles, o_stage, dx_stage):
        w_loads = [
            pltpu.make_async_copy(a, b, local.at[7 + i])
            for i, (a, b) in enumerate(((wg_all, wg_v), (wu_all, wu_v), (wd_all, wd_v)))
        ]
        for load in w_loads:
            load.start()

        def slot_of(k):
            step = k // subs
            core, y, x = 1 - (step // 2) % 2, 1 - step // 4, 1 - step % 2
            return core, y, x, k % subs

        def loads(k):
            core, y, x, sub = slot_of(k)
            slot = 4 * core + 2 * y + x
            part = pl.ds(sub * blocks, blocks)
            return [
                pltpu.make_async_copy(a.at[slot, part], b.at[k % 2], local.at[10 + 2 * i + k % 2])
                for i, (a, b) in enumerate(((x_all, x_tiles), (g_all, g_tiles)))
            ]

        for load in loads(0):
            load.start()
        if two:
            for total in (acc_g, acc_u, acc_d):
                total[...] = jnp.zeros_like(total)
        for load in w_loads:
            load.wait()

        @pl.loop(0, 8 * subs)
        def _(k):
            core, y, x, sub = slot_of(k)

            @pl.when(k + 1 < 8 * subs)
            def _():
                for load in loads(k + 1):
                    load.start()

            for load in loads(k):
                load.wait()
            start = pl.multiple_of(((4 * core + 2 * y + x) * nz + sub * blocks) * rows, tile)
            x_rows = x_tiles[k % 2].reshape(tile, features)
            g_rows = g_tiles[k % 2].reshape(tile, features)
            hidden, grad_gate, grad_up = (acts[i, pl.ds(start, tile), :] for i in range(3))
            if two:
                part = slice(cut, width)
                more = feed_forward(
                    x_rows, g_rows, wg_v[:, part], wu_v[:, part], wd_v[:, part]
                )
                acc_g[...] += dot_tn(x_rows, more[1])
                acc_u[...] += dot_tn(x_rows, more[2])
                acc_d[...] += dot_tn(g_rows, more[0])
                hidden, grad_gate, grad_up = (
                    jnp.concatenate(pair, axis=1)
                    for pair in zip((hidden, grad_gate, grad_up), more)
                )
            dx = dot_nt(grad_gate, wg_v[...]) + dot_nt(grad_up, wu_v[...])
            o = dot_nt(hidden, wd_v[...])

            @pl.when(k > 0)
            def _():
                core_before, y_before, x_before, sub_before = slot_of(k - 1)

                @pl.when(core_before == 1)
                def _():
                    scatter_dx.core_sent(2 * y_before + x_before, sub_before)
                    scatter_o.core_sent(2 * y_before + x_before, sub_before)

            @pl.when(core == 1)
            def _():
                dx_stage[...] = dx.astype(BF16).reshape(dx_stage.shape)
                scatter_dx.to_core(dx_stage, 2 * y + x, sub)
                o_stage[...] = o.astype(BF16).reshape(o_stage.shape)
                scatter_o.to_core(o_stage, 2 * y + x, sub)

            @pl.when(core == 0)
            def _():
                scatter_dx.keep(dx, 2 * y + x, sub)

                @pl.when(y == 1)
                def _():
                    @pl.loop(0, blocks)
                    def _(i):
                        scatter_dx.to_y(x, sub * blocks + blocks - 1 - i)

                scatter_o.keep(o, 2 * y + x, sub)

        if two:
            for i, total in enumerate((acc_g, acc_u, acc_d)):
                dw_part[i] = total[...].astype(BF16)

    whole = pltpu.VMEM((features, width), BF16)
    total = pltpu.VMEM((features, cut), F32)
    tiles = pltpu.VMEM((2, blocks, rows, features), BF16)
    one = pltpu.VMEM((blocks, rows, features), BF16)
    pl.run_scoped(ffn, whole, whole, whole, total, total, total, tiles, tiles, one, one)
    flow.pump(pumps[1])
    late.pump(pumps[2])
    if two:
        for copy in copies[3:]:
            copy.start()
    scatter_dx.over()
    late.pump(pumps[3])
    scatter_dx.lines()
    scatter_dx.total(acc)

    def attention(wq_v, wo_v, wkv_v, normed_v, pq, po, pk):
        scatter_q = Scatter(net, own_of(pq), other_of(pq), pq_x, pq_z, Direct())
        scatter_w = Scatter(net, own_of(po), other_of(po), po_x, po_z, Direct())
        scatter_k = Scatter(net, own_of(pk), other_of(pk), pk_x, pk_z, Direct())
        assert net.used <= counts
        ends = net.ends[-3:]
        del net.ends[-3:]
        attn_loads = [
            pltpu.make_async_copy(a, b, local.at[7 + i])
            for i, (a, b) in enumerate(
                ((wq_all, wq_v), (wo_all, wo_v), (wkv_all, wkv_v), (normed, normed_v))
            )
        ]
        for load in attn_loads:
            load.start()
        rows_in = middle[...]
        root = inverse_root(rows_in)
        grad_normed = acc[...]
        gain = lane_row(gains_all, 1, n)
        scaled = grad_normed * gain
        inner = jnp.mean(scaled * rows_in, axis=-1, keepdims=True)
        grad_middle = go[...].astype(F32) + root * (scaled - rows_in * (root * root) * inner)
        own_grad[...] = grad_middle
        gain_ffn = jnp.sum(grad_normed * rows_in * root, axis=0, keepdims=True)
        branch_rows[t] = grad_middle.astype(BF16)
        branch_g.begin()
        late.pump(pumps[4])
        for load in attn_loads:
            load.wait()
        branch_g.rest()
        scatter_o.all_to_y(1)
        grad_branch = branch_rows[...].reshape(4 * rows, features)
        chunk = 512
        for i in range(features // chunk):
            part = slice(i * chunk, (i + 1) * chunk)
            po[part, :] = dot_tn(grad_branch[:, part], context[...]).astype(BF16)
        scatter_w.begin()
        grad_context = dot_nn(grad_branch, wo_v[...]).astype(BF16)
        late.pump(pumps[5])

        allowed = allowed_pairs(lens, 4 * rows)
        key, value = keyval[:, :HD], keyval[:, HD:]
        grad_key = jnp.zeros((4 * rows, HD), F32)
        grad_value = jnp.zeros((4 * rows, HD), F32)
        factor = HD ** (-0.5)
        for h in range(heads // HD):
            lanes = slice(h * HD, (h + 1) * HD)
            probs = softmax_head(query[:, lanes], key, allowed)
            grad_head = grad_context[:, lanes]
            grad_probs = dot_nt(grad_head, value)
            inner = jnp.sum(grad_probs * probs, axis=-1, keepdims=True)
            grad_scores = (probs * (grad_probs - inner)).astype(BF16)
            grad_query[:, lanes] = (dot_nn(grad_scores, key) * factor).astype(BF16)
            grad_key += dot_tn(grad_scores, query[:, lanes]) * factor
            grad_value += dot_tn(probs.astype(BF16), grad_head)
        both = jnp.concatenate([grad_key, grad_value], axis=1).astype(BF16)
        for i in range(4):
            gkv[i] = both[:, i * quarter : (i + 1) * quarter]
        kv_s.begin()
        for i in range(features // chunk):
            part = slice(i * chunk, (i + 1) * chunk)
            pq[part, :] = dot_tn(normed_v[:, part], grad_query[...]).astype(BF16)
        scatter_q.begin()
        grad_kv = kv_s.rest().astype(BF16)
        term = dot_nt(grad_query[...], wq_v[...]) + dot_nt(grad_kv, wkv_v[...])
        qpart[...] = term.astype(BF16).reshape(qpart.shape)
        query_s.begin()
        for i in range(features // chunk):
            part = slice(i * chunk, (i + 1) * chunk)
            pk[part, :] = dot_tn(normed_v[:, part], grad_kv).astype(BF16)
        scatter_k.begin()
        late.pump(pumps[6])
        scatter_w.lines()
        scatter_o.all_to_y(0)
        scatter_q.lines()
        grad_normed = query_s.rest()

        rows_in = tok[...].astype(F32)
        root = inverse_root(rows_in)
        gain = lane_row(gains_all, 0, n)
        scaled = grad_normed * gain
        inner = jnp.mean(scaled * rows_in, axis=-1, keepdims=True)
        grad_tokens[...] = own_grad[...] + root * (scaled - rows_in * (root * root) * inner)
        gain_attn = jnp.sum(grad_normed * rows_in * root, axis=0, keepdims=True)
        for i in range(n):
            lanes = slice(i * depth, (i + 1) * depth)
            gain_parts[i, 0:1, :] = gain_attn[:, lanes]
            gain_parts[i, 1:2, :] = gain_ffn[:, lanes]
            gain_parts[i, 2:8, :] = jnp.zeros((6, depth), F32)
        gain_deal.begin()
        late.pump(pumps[7])
        scatter_k.lines()
        scatter_o.over()
        gain_land[d] = gain_parts[d]
        gain_deal.done()
        gain_sum[t] = jnp.sum(gain_land[...], axis=0)
        gain_g.begin()
        scatter_k.total(acc_k)
        k_rows[t] = acc_k[...]
        kv_g.begin()
        late.rest()
        scatter_o.lines()
        scatter_w.total(acc_w)
        grad_wo[...] = acc_w[...]
        scatter_q.total(acc_w)
        grad_wq[...] = acc_w[...]
        gain_g.rest()
        grad_gains[...] = jnp.sum(gain_sum[...], axis=0)
        kv_g.rest()
        for i in range(4):
            grad_wkv[:, i * quarter : (i + 1) * quarter] = k_rows[i]
        scatter_o.total(acc)
        block_out[...] = (middle[...] + acc[...]).astype(BF16)
        for end in ends:
            end()

    flow.rest()
    projection = pltpu.VMEM((features, heads), BF16)
    part = pltpu.VMEM((features, quarter), BF16)
    pl.run_scoped(
        attention, projection, projection, part, pltpu.VMEM((4 * rows, features), BF16),
        projection, projection, part,
    )
    for deal in deals:
        deal.done()
    for copy in copies:
        copy.wait()
    net.finish()


def params(collective_id):
    return pltpu.CompilerParams(
        collective_id=collective_id, has_side_effects=True, vmem_limit_bytes=63 * MIB
    )


PUMPS_1 = (0.12, 0.1, 0.1, 0.1, 0.06, 0.1, 0.1, 0.1, 0.1, 0.12)
PUMPS_2 = (1.0, 0.0, 0.2, 0.2, 0.1, 0.1, 0.2, 0.2)


def body(
    n, tokens, grad_out, lengths, gain_attn, gain_ffn, w_query, w_keyval, w_out, w_gate, w_up, w_down
):
    nz = n // 2
    rows, features = tokens.shape
    depth, heads = w_query.shape
    quarter = w_keyval.shape[1] // 4
    width = w_gate.shape[1] // n
    group_rows = 4 * rows
    shape = jax.ShapeDtypeStruct
    gains = jnp.concatenate(
        [gain_attn[None], gain_ffn[None], jnp.zeros((6, depth), gain_attn.dtype)]
    ).astype(F32)

    cut = width // 2 if width // 2 % 128 == 0 else width
    parts = width // cut
    tile_blocks = 256 // rows
    counts = 9 + 4 * 3 * nz + 2 * (5 * nz + 4) + 3 * parts * n
    full = shape((features, width), BF16)
    part = shape((features, cut), BF16)
    wide = shape((8, nz, rows, features), BF16)
    all_rows = 4 * n * rows
    (
        wg_all, wu_all, wd_all, x_all, g_all, wq_all, wkv_all, wo_all, gains_all,
        query, keyval, context, normed, middle, acts, dwg, dwu, dwd,
    ) = pl.pallas_call(
        functools.partial(first_kernel, n, counts, PUMPS_1),
        out_shape=(
            full, full, full, wide, wide,
            shape((features, heads), BF16),
            shape((features, quarter), BF16),
            shape((features, heads), BF16),
            shape((8 * n, depth), F32),
            shape((group_rows, heads), BF16),
            shape((group_rows, 2 * HD), BF16),
            shape((group_rows, heads), BF16),
            shape((group_rows, features), BF16),
            shape((rows, features), F32),
            shape((3, all_rows, cut), BF16),
            part, part, part,
        ),
        in_specs=[SMEM] + [ANY] * 9,
        out_specs=(ANY,) * 9 + (VMEM,) * 9,
        scratch_shapes=[
            pltpu.SemaphoreType.DMA((counts,)),
            pltpu.SemaphoreType.DMA((counts,)),
            pltpu.SemaphoreType.DMA((9,)),
            pltpu.VMEM((features, heads), BF16),
            pltpu.VMEM((features, quarter), BF16),
            pltpu.VMEM((features, heads), BF16),
            pltpu.VMEM((8 * n, depth), F32),
            pltpu.VMEM((4, rows, features), BF16),
            pltpu.VMEM((4, group_rows, quarter), BF16),
            pltpu.VMEM((4, rows, features), BF16),
            pltpu.VMEM((2, rows, features), BF16),
            pltpu.VMEM((rows, features), BF16),
            pltpu.VMEM((rows, features), BF16),
            pltpu.VMEM((3, features, cut), BF16),
            pltpu.VMEM((tile_blocks, rows, features), BF16),
            pltpu.VMEM((tile_blocks, rows, features), BF16),
        ]
        + [pltpu.VMEM((features, cut), F32)] * 3,
        compiler_params=params(0),
        name="forward",
    )(lengths, tokens, grad_out, gains, w_query, w_keyval, w_out, w_gate, w_up, w_down)

    staged = n > 8
    subs = nz // tile_blocks
    counts = 2 * (4 * subs + 5 * nz) + 3 * 3 * nz + 15 + n + 3 * parts * n
    landing = [
        shape((4, nz, rows, features), BF16),
        shape((2, nz, rows, features), BF16),
        shape((nz, rows, features), BF16),
        shape((nz + 1, rows, features), BF16),
    ] * 2
    out_shape = [
        shape((rows, features), BF16),
        shape((rows, features), F32),
        shape((8, depth), F32),
        shape((depth, heads), F32),
        shape((depth, 4 * quarter), F32),
        shape((depth, heads), F32),
        shape((depth, n * width), BF16),
        shape((depth, n * width), BF16),
        shape((depth, n * width), BF16),
    ]
    out_specs = [VMEM] * 6 + [ANY] * 3
    in_vmem = []
    if staged:
        out_shape += landing
        out_specs += [ANY] * len(landing)
    else:
        in_vmem = [pltpu.VMEM(place.shape, place.dtype) for place in landing]

    def reduced(columns):
        return [
            pltpu.VMEM((nz, depth, columns), BF16),
            pltpu.VMEM((nz + 1, depth, columns), BF16),
        ]

    results = pl.pallas_call(
        functools.partial(second_kernel, n, counts, staged, PUMPS_2),
        out_shape=tuple(out_shape),
        in_specs=[SMEM, ANY, ANY, VMEM] + [ANY] * 10 + [VMEM] * 7,
        out_specs=tuple(out_specs),
        scratch_shapes=in_vmem
        + [
            pltpu.SemaphoreType.DMA((counts,)),
            pltpu.SemaphoreType.DMA((counts,)),
            pltpu.SemaphoreType.DMA((14,)),
            pltpu.VMEM((tile_blocks if staged else 1, rows, features), BF16),
            pltpu.VMEM((3, features, cut if parts > 1 else 128), BF16),
            pltpu.VMEM((rows, features), F32),
            pltpu.VMEM((4, rows, features), BF16),
            pltpu.VMEM((4, group_rows, quarter), BF16),
            pltpu.VMEM((2, group_rows, quarter), BF16),
            pltpu.VMEM((group_rows, quarter), BF16),
            pltpu.VMEM((4, rows, features), BF16),
            pltpu.VMEM((2, rows, features), BF16),
            pltpu.VMEM((rows, features), BF16),
        ]
        + reduced(heads)
        + reduced(heads)
        + reduced(quarter)
        + [
            pltpu.VMEM((4, depth, quarter), F32),
            pltpu.VMEM((depth, heads), F32),
            pltpu.VMEM((depth, quarter), F32),
            pltpu.VMEM((n, 8, depth), F32),
            pltpu.VMEM((n, 8, depth), F32),
            pltpu.VMEM((4, 8, depth), F32),
            pltpu.VMEM((group_rows, heads), BF16),
            pltpu.VMEM((rows, features), F32),
        ],
        compiler_params=params(1),
        name="backward",
    )(
        lengths, x_all, g_all, acts, wg_all, wu_all, wd_all, dwg, dwu, dwd,
        wq_all, wkv_all, wo_all, normed,
        tokens, grad_out, gains_all, query, keyval, context, middle,
    )
    block_out, grad_tokens, grad_gains, grad_wq, grad_wkv, grad_wo, grad_wg, grad_wu, grad_wd = (
        results[:9]
    )
    return (
        block_out,
        grad_tokens,
        grad_gains[0],
        grad_gains[1],
        grad_wq,
        grad_wkv,
        grad_wo,
        grad_wg.astype(F32),
        grad_wu.astype(F32),
        grad_wd.astype(F32),
    )


def solution(mesh):
    rows = P(("dp", "tensor"), None)
    both = P("dp", "tensor")
    return jax.shard_map(
        functools.partial(body, mesh.shape["dp"]),
        mesh=mesh,
        in_specs=(rows, rows, P("dp", None), P("dp"), P("dp"), both, P("dp", None), both, both, both, both),
        out_specs=(rows, rows, P("dp"), P("dp"), both, P("dp", None), both, both, both, both),
        check_vma=False,
    )
```

time: 595 us -> 520 us (0.87)
  Pallas kernels: 577 us -> 502 us
    pallas_call x3 -> x2, Pallas kernels: 577 us -> 502 us  [the longest x1 266 us: body(): pl.pallas_call(functools.partial(second_kernel, n, counts, staged, PUMPS_...]
where the time goes in v2:
time: 520 us; the launch traced here: 519 us
  Pallas kernels  502 us (97%)
  other arithmetic  9.92 us (2%)
  local copies, waits for them, and re-layouts  6.64 us (1%)
    pallas_call x1, Pallas kernels, body(): pl.pallas_call(functools.partial(second_kernel, n, counts, staged, PUMPS_...  266 us
    pallas_call x1, Pallas kernels, body(): pl.pallas_call(functools.partial(first_kernel, n, counts, PUMPS_1), out_s...  236 us

profile of v2, /device:TPU:0, one launch (start us, length us, event | category | flops | bytes accessed | tf_op | source)
XLA Modules:
  0.0 519.4 jit_solution(1502543194955840383)
XLA Ops:
  0.7 0.1 pad.2.clone
  0.7 0.7 broadcast_in_dim.9
  1.4 0.7 broadcast_in_dim.10
  2.0 0.7 maximum_convert_fusion.gains
  2.7 235.8 %forward.1 = (bf16[2048,512]{1,0:T(8,128)(2,1)}, bf16[2048,512]{1,0:T(8,128)(2,1)}, bf16[2048,512]{1,0:T(8,128)(2,1)}, bf16[8,4,64,2048]{3,2,1,0:T(8,128)(2,1)},...) custom-call(s32[1,3]{1,0:T(1,128)} %lens.3, ...), custom_call_target="tpu_custom_call" | custom-call | tf_op jit(solution)/shard_map/forward/pallas_call | solution.py:1158
  238.5 266.3 %backward.1 = (bf16[64,2048]{1,0:T(8,128)(2,1)}, f32[64,2048]{1,0:T(8,128)}, f32[8,256]{1,0:T(8,128)}, f32[256,512]{1,0:T(8,128)}, f32[256,512]{1,0:T(8,128)}, /...) custom-call(s32[1,3]{1,0:T(1,128)} %lens.3, ...), custom_call_target="tpu_custom_call" | custom-call | tf_op jit(solution)/shard_map/backward/pallas_call | solution.py:1233
  504.9 1.3 fusion
  506.2 0.0 copy-start.1
  506.2 4.2 convert_element_type.13
  510.5 0.0 copy-done.1
  510.5 0.0 copy-start
  510.5 2.5 convert_element_type.14
  513.0 0.0 copy-done
  513.0 0.0 copy-start.6
  513.0 0.0 copy-start.5
  513.0 0.0 copy-start.4
  513.0 2.5 convert_element_type.15
  515.5 0.0 copy-done.6
  515.5 0.0 copy-start.3
  515.5 0.0 copy-start.2
  515.5 0.7 copy.26
  516.2 0.0 copy-done.5
  516.2 0.8 copy.27
  517.0 0.0 copy-done.4
  517.0 0.8 copy.28
  517.8 0.0 copy-done.3
  517.8 0.8 copy.29
  518.6 0.0 copy-done.2
  518.6 0.8 copy.30
  (1 shorter events, 0.0 us)
Async XLA Ops:
  506.2 4.3 copy-start.1
  510.5 2.5 copy-start
  513.0 2.5 copy-start.6
  513.0 3.2 copy-start.5
  513.0 4.0 copy-start.4
  515.5 2.3 copy-start.3
  515.5 3.1 copy-start.2

commit v3 on v2

--- a/solution.py
+++ b/solution.py
@@ -233,8 +233,8 @@
 
 
 class WideSpread:
-    def __init__(self, net, buf):
-        self.net, self.buf = net, buf
+    def __init__(self, net, buf, late_x=False):
+        self.net, self.buf, self.late_x = net, buf, late_x
         self.zk, self.xk = net.take(2 * net.nz), net.take(net.nz)
         self.yk, self.ck = net.take(2 * net.nz), net.take(4)
         net.ends.append(self.end)
@@ -254,7 +254,16 @@
                 net.start(src, buf.at[0, zb], self.zk + net.nz + zb, net.dp(net.d - 2))
 
         net.start(src, buf.at[2, zb], self.yk + zb, net.tensor(net.ty))
-        net.start(src, buf.at[1, zb], self.xk + zb, net.dp(net.dx))
+        if not self.late_x:
+            net.start(src, buf.at[1, zb], self.xk + zb, net.dp(net.dx))
+
+    def send_x(self):
+        net = self.net
+
+        @pl.loop(0, net.nz)
+        def _(k):
+            zb = (net.z + k) % net.nz
+            net.start(self.buf.at[0, zb], self.buf.at[1, zb], self.xk + zb, net.dp(net.dx))
 
     def begin(self, own):
         self.onward(own, self.net.z, True, True)
@@ -354,19 +363,53 @@
 
 
 class Flow:
-    def __init__(self, deals):
-        self.todo = [(deal, m) for deal in deals for m in range(1, deal.net.n)]
-        self.total, self.gone, self.share = len(self.todo), 0, 0.0
-
-    def pump(self, share):
+    def __init__(self, n, groups, even_first):
+        self.todo = []
+        for deals in groups:
+            for parity in (0, 1) if even_first else (1, 0):
+                self.todo += [(deal, m) for deal in deals for m in range(1, n) if m % 2 == parity]
+        self.gone, self.share = 0, 0.0
+
+    def pump(self, share, limit=None):
         self.share += share
-        upto = min(self.total, round(self.share * self.total))
+        upto = min(round(self.share * len(self.todo)), len(self.todo) if limit is None else limit)
         for deal, m in self.todo[self.gone : upto]:
             deal.send(m)
         self.gone = max(upto, self.gone)
 
     def rest(self):
         self.pump(1.0)
+
+
+class Columns:
+    def __init__(self, net, parts, land):
+        self.net, self.parts, self.land = net, parts, land
+        self.deal = Deal(net, lambda to: parts.at[to], lambda frm: land.at[net.t, frm])
+        self.over = TensorGather(net, lambda i: land.at[i])
+
+    def begin(self, rows):
+        depth = self.parts.shape[2]
+        for i in range(self.net.n):
+            self.parts[i] = rows[:, i * depth : (i + 1) * depth]
+        self.land[self.net.t, self.net.d] = self.parts[self.net.d]
+        self.deal.begin()
+
+    def gather(self):
+        self.deal.done()
+        self.over.begin()
+
+    def rest(self):
+        self.over.rest()
+
+    def times(self, other, acc):
+        n = self.net.n
+        depth = self.parts.shape[2]
+        acc[...] = jnp.zeros_like(acc)
+
+        @pl.loop(0, n)
+        def _(i):
+            mine = self.land[:, i].reshape(-1, depth)
+            acc[...] += dot_tn(mine, row_block(n, other, i)[...])
 
 
 class Scatter:
@@ -397,42 +440,39 @@
         net.landed(self.xl.at[zb], self.xk + zb)
         self.add(self.own(zb), self.xl.at[zb])
 
+    def line_step(self, k):
+        net = self.net
+        nz = net.nz
+        far = nz - 1 - k
+
+        @pl.when(far > net.z)
+        def _():
+            self.meet(far)
+            here = self.own(far)
+
+            @pl.when(net.z > 0)
+            def _():
+                net.landed(self.zl.at[far], self.rk + far)
+                self.add(here, self.zl.at[far])
+
+            net.start(here, self.zl.at[far], self.rk + far, net.dp(net.d + 2))
+
+        @pl.when(k < net.z)
+        def _():
+            self.meet(k)
+            here = self.own(k)
+
+            @pl.when(net.z < nz - 1)
+            def _():
+                net.landed(self.zl.at[k], self.lk + k)
+                self.add(here, self.zl.at[k])
+
+            last = (k == net.z - 1).astype(jnp.int32)
+            net.start(here, self.zl.at[last * nz + (1 - last) * k], self.lk + k, net.dp(net.d - 2))
+
     def lines(self):
-        net = self.net
-        nz = net.nz
-
-        @pl.loop(0, nz - 1)
-        def _(k):
-            far = nz - 1 - k
-
-            @pl.when(far > net.z)
-            def _():
-                self.meet(far)
-                here = self.own(far)
-
-                @pl.when(net.z > 0)
-                def _():
-                    net.landed(self.zl.at[far], self.rk + far)
-                    self.add(here, self.zl.at[far])
-
-                net.start(here, self.zl.at[far], self.rk + far, net.dp(net.d + 2))
-
-            @pl.when(k < net.z)
-            def _():
-                self.meet(k)
-                here = self.own(k)
-
-                @pl.when(net.z < nz - 1)
-                def _():
-                    net.landed(self.zl.at[k], self.lk + k)
-                    self.add(here, self.zl.at[k])
-
-                last = (k == net.z - 1).astype(jnp.int32)
-                net.start(
-                    here, self.zl.at[last * nz + (1 - last) * k], self.lk + k, net.dp(net.d - 2)
-                )
-
-        self.meet(net.z)
+        pl.loop(0, self.net.nz - 1)(self.line_step)
+        self.meet(self.net.z)
 
     def total(self, acc):
         net, mem = self.net, self.mem
@@ -606,6 +646,42 @@
 
 def lanes_at(start, size):
     return pl.ds(pl.multiple_of(start, 128), size)
+
+
+def weight_blocks(columns, acts, cols):
+    x_cols, g_cols = columns
+    return (
+        dot_tn(x_cols, acts[1, :, cols]),
+        dot_tn(x_cols, acts[2, :, cols]),
+        dot_tn(g_cols, acts[0, :, cols]),
+    )
+
+
+def by_columns(x_all, g_all, x_cols, g_cols, sems, use):
+    features = x_all.shape[3]
+    chunk = x_cols.shape[4]
+    count = features // chunk
+
+    def loads(c):
+        lanes = lanes_at(c * chunk, chunk)
+        return [
+            pltpu.make_async_copy(a.at[:, :, :, lanes], b.at[c % 2], sems.at[2 * i + c % 2])
+            for i, (a, b) in enumerate(((x_all, x_cols), (g_all, g_cols)))
+        ]
+
+    for load in loads(0):
+        load.start()
+
+    @pl.loop(0, count)
+    def _(c):
+        @pl.when(c + 1 < count)
+        def _():
+            for load in loads(c + 1):
+                load.start()
+
+        for load in loads(c):
+            load.wait()
+        use(pl.multiple_of(c * chunk, chunk), [b[c % 2].reshape(-1, chunk) for b in (x_cols, g_cols)])
 
 
 def first_kernel(
@@ -633,7 +709,7 @@
     branch_s = TensorScatter(net, branch, branch_c, branch_y)
     first_w = Spread(net, [wq_all, wkv_all, gains_all], block)
     second_w = Spread(net, [wo_all], block)
-    spread_g = WideSpread(net, g_all)
+    spread_g = WideSpread(net, g_all, late_x=True)
     spread_x = WideSpread(net, x_all)
     deals = [
         Deal(
@@ -645,7 +721,7 @@
         for w, full in ((wg, wg_all), (wu, wu_all), (wd, wd_all))
     ]
     assert net.used <= counts
-    flow = Flow(deals)
+    flow = Flow(n, [deals[:3], deals[3:]], True)
 
     own_copies = [
         (tok, group.at[t]),
@@ -671,8 +747,11 @@
     first_w.begin()
     flow.pump(pumps[0])
     own_copies[4].wait()
+    own_copies[5].wait()
     tokens_g.rest()
     second_w.begin()
+    spread_g.begin(go)
+    flow.pump(pumps[1])
 
     @pl.loop(1, net.nz)
     def _(h):
@@ -682,42 +761,43 @@
         def _():
             second_w.hop(h - 1)
 
-    flow.pump(pumps[1])
+        spread_g.hop(h)
+
+    flow.pump(pumps[2])
     inputs = group[...].reshape(4 * rows, features).astype(F32)
     root = inverse_root(inputs)
     first_w.cross()
     second_w.hop(net.nz - 1)
-    spread_g.begin(go)
-    flow.pump(pumps[2])
+    spread_g.send_x()
+    flow.pump(pumps[3])
     gain = lane_row(gains_all, 0, n)
     normed = (inputs * root * gain).astype(BF16)
     normed_out[...] = normed
     kv_parts[t] = dot_nn(normed, wkv_all[...]).astype(BF16)
     kv_g.begin()
     query_out[...] = dot_nn(normed, wq_all[...]).astype(BF16)
-    spread_g.hop(1)
+    flow.pump(pumps[4])
     kv_g.rest()
     for i in range(4):
         keyval_out[:, i * quarter : (i + 1) * quarter] = kv_parts[i]
     allowed = allowed_pairs(lens, 4 * rows)
-    flow.pump(pumps[3])
     for h in range(query_out.shape[1] // HD):
         lanes = slice(h * HD, (h + 1) * HD)
         probs = softmax_head(query_out[:, lanes], keyval_out[:, :HD], allowed).astype(BF16)
         context_out[:, lanes] = dot_nn(probs, keyval_out[:, HD:]).astype(BF16)
-    pl.loop(2, net.nz)(spread_g.hop)
+    flow.pump(pumps[5])
     second_w.cross()
     branch[...] = dot_nt(context_out[...], wo_all[...]).astype(BF16).reshape(branch.shape)
     branch_s.begin()
-    flow.pump(pumps[4])
-    spread_g.cross()
+    flow.pump(pumps[6])
     middle = group[t].astype(F32) + branch_s.rest()
     middle_out[...] = middle
     own_normed[...] = (middle * inverse_root(middle) * lane_row(gains_all, 1, n)).astype(BF16)
     own_x = pltpu.make_async_copy(own_normed, x_all.at[0, net.z], local.at[0])
     own_x.start()
     spread_x.begin(own_normed)
-    flow.pump(pumps[5])
+    spread_g.cross()
+    flow.pump(pumps[7])
     outs = [
         pltpu.make_async_copy(a, b, local.at[1 + i])
         for i, (a, b) in enumerate(
@@ -731,20 +811,19 @@
     ]
     for copy in outs:
         copy.start()
-    own_copies[5].wait()
     own_x.wait()
     spread_x.hops()
-    flow.pump(pumps[6])
+    flow.pump(pumps[8])
     spread_x.core(0)
     spread_g.core(0)
+    spread_g.core(1)
     spread_x.cross()
-    flow.pump(pumps[7])
+    flow.pump(pumps[9])
     spread_x.core(1)
-    spread_g.core(1)
     for x in range(2):
         spread_g.over(x)
         spread_g.core(2 + x)
-    flow.pump(pumps[8])
+    flow.pump(pumps[10])
     for slot in range(4):
         spread_g.core_done(slot)
 
@@ -758,13 +837,19 @@
         acc[...] = jnp.zeros_like(acc)
     for i, full in enumerate((wg_all, wu_all, wd_all)):
         pltpu.make_async_copy(full.at[:, pl.ds(0, cut)], w_part.at[i], local.at[5 + i]).wait()
-    flow.pump(pumps[9])
+    flow.pump(pumps[11])
     tile_blocks = x_tile.shape[0]
     tile = tile_blocks * rows
 
     @pl.loop(0, 8)
     def _(k):
         slot = k % 2 + 4 * ((k // 2) % 2) + 2 * (k // 4)
+        for at in range(1, 8):
+
+            @pl.when(k == at)
+            def _():
+                flow.pump(pumps[11 + at])
+
         for at, slot_from in ((2, 0), (3, 1), (6, 2), (7, 3)):
 
             @pl.when(k == at)
@@ -813,22 +898,22 @@
 
 def second_kernel(
     n, counts, staged, pumps,
-    lens, x_all, g_all, acts, wg_all, wu_all, wd_all, dwg, dwu, dwd,
+    lens, x_all, g_all, acts_first, wg_all, wu_all, wd_all, dwg, dwu, dwd,
     wq_all, wkv_all, wo_all, normed,
     tok, go, gains_all, query, keyval, context, middle,
     block_out, grad_tokens, grad_gains, grad_wq, grad_wkv, grad_wo, grad_wg, grad_wu, grad_wd,
     dx_c, dx_y, dx_x, dx_z, o_c, o_y, o_x, o_z,
     send, recv, local, stage, dw_part,
     acc, branch_rows, gkv, gkv_c, gkv_y, qpart, qpart_c, qpart_y,
-    pq_x, pq_z, po_x, po_z, pk_x, pk_z, k_rows, acc_w, acc_k,
-    gain_parts, gain_land, gain_sum, grad_query, own_grad,
+    context_all, query_all, key_all, norm_parts, norm_land, branch_parts, branch_land, k_rows,
+    gain_parts, gain_land, gain_sum, grad_query, normed_own,
 ):
     net = Net(n, send, recv)
     d, t = net.d, net.t
     nz = net.nz
     depth, heads = grad_wq.shape
     features, width = wg_all.shape
-    cut = acts.shape[2]
+    cut = acts_first.shape[2]
     two = cut < width
     rows = tok.shape[0]
     quarter = wkv_all.shape[1]
@@ -838,12 +923,6 @@
 
     def block(buf, idx):
         return row_block(n, buf, idx)
-
-    def own_of(buf):
-        return lambda zb: block(buf, 2 * zb + net.x)
-
-    def other_of(buf):
-        return lambda zb: block(buf, 2 * zb + 1 - net.x)
 
     mem = Staged(stage, local.at[0]) if staged else Direct()
     scatter_dx = WideScatter(net, dx_c, dx_y, dx_x, dx_z, mem, subs)
@@ -854,6 +933,11 @@
     kv_g = TensorGather(net, lambda i: k_rows.at[i])
     gain_deal = Deal(net, lambda to: gain_parts.at[to], lambda frm: gain_land.at[frm])
     gain_g = TensorGather(net, lambda i: gain_sum.at[i])
+    context_s = Spread(net, [context_all], block)
+    query_g = Spread(net, [query_all], block)
+    key_g = Spread(net, [key_all], block)
+    norm_cols = Columns(net, norm_parts, norm_land)
+    branch_cols = Columns(net, branch_parts, branch_land)
     outs = (grad_wg, grad_wu, grad_wd)
     deals = [
         Deal(
@@ -872,136 +956,142 @@
             )
             for i, out in enumerate(outs)
         ]
-    flow = Flow(deals[:3])
-    late = Flow(deals[3:])
+    flow = Flow(n, [deals[:3], deals[3:]], False)
+    first_half = 3 * (n - 1)
     copies = [
         pltpu.make_async_copy(deal.src(d), deal.dst(d), local.at[1 + i])
         for i, deal in enumerate(deals)
     ]
     for copy in copies[:3]:
         copy.start()
+    own_rows = pltpu.make_async_copy(
+        normed.at[pl.ds(pl.multiple_of(t * rows, rows), rows)], normed_own, local.at[6]
+    )
+    own_rows.start()
+    block(context_all, d)[...] = context[...]
     net.greet()
-    flow.pump(pumps[0])
-
-    def ffn(wg_v, wu_v, wd_v, acc_g, acc_u, acc_d, x_tiles, g_tiles, o_stage, dx_stage):
+    context_s.begin()
+    own_rows.wait()
+    norm_cols.begin(normed_own[...])
+    flow.pump(pumps[0], first_half)
+
+    def ffn(wg_v, wu_v, wd_v, acts, x_tiles, g_tiles, x_cols, g_cols, one):
         w_loads = [
             pltpu.make_async_copy(a, b, local.at[7 + i])
-            for i, (a, b) in enumerate(((wg_all, wg_v), (wu_all, wu_v), (wd_all, wd_v)))
+            for i, (a, b) in enumerate(
+                (
+                    (wg_all, wg_v), (wu_all, wu_v), (wd_all, wd_v),
+                    (acts_first, acts.at[:, :, pl.ds(0, cut)]),
+                )
+            )
         ]
         for load in w_loads:
             load.start()
 
-        def slot_of(k):
+        def place(k):
             step = k // subs
-            core, y, x = 1 - (step // 2) % 2, 1 - step // 4, 1 - step % 2
-            return core, y, x, k % subs
+            core, y, x, sub = 1 - (step // 2) % 2, 1 - step // 4, 1 - step % 2, k % subs
+            start = pl.multiple_of(((4 * core + 2 * y + x) * nz + sub * blocks) * rows, tile)
+            return core, y, x, sub, pl.ds(start, tile)
 
         def loads(k):
-            core, y, x, sub = slot_of(k)
-            slot = 4 * core + 2 * y + x
+            core, y, x, sub, _ = place(k)
             part = pl.ds(sub * blocks, blocks)
             return [
-                pltpu.make_async_copy(a.at[slot, part], b.at[k % 2], local.at[10 + 2 * i + k % 2])
+                pltpu.make_async_copy(
+                    a.at[4 * core + 2 * y + x, part], b.at[k % 2], local.at[11 + 2 * i + k % 2]
+                )
                 for i, (a, b) in enumerate(((x_all, x_tiles), (g_all, g_tiles)))
             ]
 
-        for load in loads(0):
-            load.start()
+        def hand_over(scatter, value, k):
+            core, y, x, sub, _ = place(k)
+
+            @pl.when(k > 0)
+            def _():
+                core_before, y_before, x_before, sub_before, _ = place(k - 1)
+
+                @pl.when(core_before == 1)
+                def _():
+                    scatter.core_sent(2 * y_before + x_before, sub_before)
+
+            @pl.when(core == 1)
+            def _():
+                one[...] = value.astype(BF16).reshape(one.shape)
+                scatter.to_core(one, 2 * y + x, sub)
+
+            @pl.when(core == 0)
+            def _():
+                scatter.keep(value, 2 * y + x, sub)
+
         if two:
-            for total in (acc_g, acc_u, acc_d):
-                total[...] = jnp.zeros_like(total)
+            for load in loads(0):
+                load.start()
         for load in w_loads:
             load.wait()
+        more = slice(cut, width)
 
         @pl.loop(0, 8 * subs)
         def _(k):
-            core, y, x, sub = slot_of(k)
-
-            @pl.when(k + 1 < 8 * subs)
-            def _():
-                for load in loads(k + 1):
-                    load.start()
-
-            for load in loads(k):
-                load.wait()
-            start = pl.multiple_of(((4 * core + 2 * y + x) * nz + sub * blocks) * rows, tile)
-            x_rows = x_tiles[k % 2].reshape(tile, features)
-            g_rows = g_tiles[k % 2].reshape(tile, features)
-            hidden, grad_gate, grad_up = (acts[i, pl.ds(start, tile), :] for i in range(3))
+            core, y, x, sub, here = place(k)
             if two:
-                part = slice(cut, width)
-                more = feed_forward(
-                    x_rows, g_rows, wg_v[:, part], wu_v[:, part], wd_v[:, part]
+
+                @pl.when(k + 1 < 8 * subs)
+                def _():
+                    for load in loads(k + 1):
+                        load.start()
+
+                for load in loads(k):
+                    load.wait()
+                done = feed_forward(
+                    x_tiles[k % 2].reshape(tile, features),
+                    g_tiles[k % 2].reshape(tile, features),
+                    wg_v[:, more], wu_v[:, more], wd_v[:, more],
                 )
-                acc_g[...] += dot_tn(x_rows, more[1])
-                acc_u[...] += dot_tn(x_rows, more[2])
-                acc_d[...] += dot_tn(g_rows, more[0])
-                hidden, grad_gate, grad_up = (
-                    jnp.concatenate(pair, axis=1)
-                    for pair in zip((hidden, grad_gate, grad_up), more)
-                )
-            dx = dot_nt(grad_gate, wg_v[...]) + dot_nt(grad_up, wu_v[...])
-            o = dot_nt(hidden, wd_v[...])
-
-            @pl.when(k > 0)
-            def _():
-                core_before, y_before, x_before, sub_before = slot_of(k - 1)
-
-                @pl.when(core_before == 1)
-                def _():
-                    scatter_dx.core_sent(2 * y_before + x_before, sub_before)
-                    scatter_o.core_sent(2 * y_before + x_before, sub_before)
-
-            @pl.when(core == 1)
-            def _():
-                dx_stage[...] = dx.astype(BF16).reshape(dx_stage.shape)
-                scatter_dx.to_core(dx_stage, 2 * y + x, sub)
-                o_stage[...] = o.astype(BF16).reshape(o_stage.shape)
-                scatter_o.to_core(o_stage, 2 * y + x, sub)
-
-            @pl.when(core == 0)
-            def _():
-                scatter_dx.keep(dx, 2 * y + x, sub)
-
-                @pl.when(y == 1)
-                def _():
-                    @pl.loop(0, blocks)
-                    def _(i):
-                        scatter_dx.to_y(x, sub * blocks + blocks - 1 - i)
-
-                scatter_o.keep(o, 2 * y + x, sub)
-
+                for i, act in enumerate(done):
+                    acts[i, here, more] = act
+            dx = dot_nt(acts[1, here, :], wg_v[...]) + dot_nt(acts[2, here, :], wu_v[...])
+            hand_over(scatter_dx, dx, k)
+            @pl.when((core == 0) & (y == 1))
+            def _():
+                @pl.loop(0, blocks)
+                def _(i):
+                    scatter_dx.to_y(x, sub * blocks + blocks - 1 - i)
+
+        @pl.loop(0, 8 * subs)
+        def _(k):
+            hand_over(scatter_o, dot_nt(acts[0, place(k)[4], :], wd_v[...]), k)
+
+        scatter_dx.over()
         if two:
-            for i, total in enumerate((acc_g, acc_u, acc_d)):
-                dw_part[i] = total[...].astype(BF16)
-
-    whole = pltpu.VMEM((features, width), BF16)
-    total = pltpu.VMEM((features, cut), F32)
+
+            def second_gradients(start, columns):
+                for i, block in enumerate(weight_blocks(columns, acts, more)):
+                    dw_part[i, pl.ds(start, block.shape[0]), :] = block.astype(BF16)
+
+            by_columns(x_all, g_all, x_cols, g_cols, local.at[pl.ds(11, 4)], second_gradients)
+
+    weights = pltpu.VMEM((features, width), BF16)
     tiles = pltpu.VMEM((2, blocks, rows, features), BF16)
-    one = pltpu.VMEM((blocks, rows, features), BF16)
-    pl.run_scoped(ffn, whole, whole, whole, total, total, total, tiles, tiles, one, one)
-    flow.pump(pumps[1])
-    late.pump(pumps[2])
+    chunks = pltpu.VMEM((2, 8, nz, rows, 256), BF16)
+    pl.run_scoped(
+        ffn, weights, weights, weights, pltpu.VMEM((3, 8 * nz * rows, width), BF16),
+        tiles, tiles, chunks, chunks, pltpu.VMEM((blocks, rows, features), BF16),
+    )
     if two:
         for copy in copies[3:]:
             copy.start()
-    scatter_dx.over()
-    late.pump(pumps[3])
+    flow.pump(pumps[1])
+    scatter_o.all_to_y(1)
     scatter_dx.lines()
+    flow.pump(pumps[2])
+    context_s.hop(1)
     scatter_dx.total(acc)
 
-    def attention(wq_v, wo_v, wkv_v, normed_v, pq, po, pk):
-        scatter_q = Scatter(net, own_of(pq), other_of(pq), pq_x, pq_z, Direct())
-        scatter_w = Scatter(net, own_of(po), other_of(po), po_x, po_z, Direct())
-        scatter_k = Scatter(net, own_of(pk), other_of(pk), pk_x, pk_z, Direct())
-        assert net.used <= counts
-        ends = net.ends[-3:]
-        del net.ends[-3:]
+    def attention(wq_v, wo_v, wkv_v):
         attn_loads = [
             pltpu.make_async_copy(a, b, local.at[7 + i])
-            for i, (a, b) in enumerate(
-                ((wq_all, wq_v), (wo_all, wo_v), (wkv_all, wkv_v), (normed, normed_v))
-            )
+            for i, (a, b) in enumerate(((wq_all, wq_v), (wo_all, wo_v), (wkv_all, wkv_v)))
         ]
         for load in attn_loads:
             load.start()
@@ -1012,23 +1102,23 @@
         scaled = grad_normed * gain
         inner = jnp.mean(scaled * rows_in, axis=-1, keepdims=True)
         grad_middle = go[...].astype(F32) + root * (scaled - rows_in * (root * root) * inner)
-        own_grad[...] = grad_middle
-        gain_ffn = jnp.sum(grad_normed * rows_in * root, axis=0, keepdims=True)
         branch_rows[t] = grad_middle.astype(BF16)
         branch_g.begin()
-        late.pump(pumps[4])
+        grad_tokens[...] = grad_middle
+        gain_ffn = jnp.sum(grad_normed * rows_in * root, axis=0, keepdims=True)
+        branch_cols.begin(grad_middle.astype(BF16))
+        flow.pump(pumps[3])
         for load in attn_loads:
             load.wait()
         branch_g.rest()
-        scatter_o.all_to_y(1)
+        scatter_o.all_to_y(0)
+        context_s.hop(2)
         grad_branch = branch_rows[...].reshape(4 * rows, features)
-        chunk = 512
-        for i in range(features // chunk):
-            part = slice(i * chunk, (i + 1) * chunk)
-            po[part, :] = dot_tn(grad_branch[:, part], context[...]).astype(BF16)
-        scatter_w.begin()
         grad_context = dot_nn(grad_branch, wo_v[...]).astype(BF16)
-        late.pump(pumps[5])
+        pl.loop(3, nz)(context_s.hop)
+        scatter_o.over()
+        norm_cols.gather()
+        flow.pump(pumps[4])
 
         allowed = allowed_pairs(lens, 4 * rows)
         key, value = keyval[:, :HD], keyval[:, HD:]
@@ -1045,26 +1135,24 @@
             grad_query[:, lanes] = (dot_nn(grad_scores, key) * factor).astype(BF16)
             grad_key += dot_tn(grad_scores, query[:, lanes]) * factor
             grad_value += dot_tn(probs.astype(BF16), grad_head)
+        block(query_all, d)[...] = grad_query[...]
+        query_g.begin()
         both = jnp.concatenate([grad_key, grad_value], axis=1).astype(BF16)
         for i in range(4):
             gkv[i] = both[:, i * quarter : (i + 1) * quarter]
         kv_s.begin()
-        for i in range(features // chunk):
-            part = slice(i * chunk, (i + 1) * chunk)
-            pq[part, :] = dot_tn(normed_v[:, part], grad_query[...]).astype(BF16)
-        scatter_q.begin()
+        flow.pump(pumps[5])
+        term = dot_nt(grad_query[...], wq_v[...])
         grad_kv = kv_s.rest().astype(BF16)
-        term = dot_nt(grad_query[...], wq_v[...]) + dot_nt(grad_kv, wkv_v[...])
+        block(key_all, d)[...] = grad_kv
+        key_g.begin()
+        term += dot_nt(grad_kv, wkv_v[...])
         qpart[...] = term.astype(BF16).reshape(qpart.shape)
         query_s.begin()
-        for i in range(features // chunk):
-            part = slice(i * chunk, (i + 1) * chunk)
-            pk[part, :] = dot_tn(normed_v[:, part], grad_kv).astype(BF16)
-        scatter_k.begin()
-        late.pump(pumps[6])
-        scatter_w.lines()
-        scatter_o.all_to_y(0)
-        scatter_q.lines()
+        branch_cols.gather()
+        query_g.hop(1)
+        key_g.hop(1)
+        flow.pump(pumps[6])
         grad_normed = query_s.rest()
 
         rows_in = tok[...].astype(F32)
@@ -1072,7 +1160,7 @@
         gain = lane_row(gains_all, 0, n)
         scaled = grad_normed * gain
         inner = jnp.mean(scaled * rows_in, axis=-1, keepdims=True)
-        grad_tokens[...] = own_grad[...] + root * (scaled - rows_in * (root * root) * inner)
+        grad_tokens[...] += root * (scaled - rows_in * (root * root) * inner)
         gain_attn = jnp.sum(grad_normed * rows_in * root, axis=0, keepdims=True)
         for i in range(n):
             lanes = slice(i * depth, (i + 1) * depth)
@@ -1080,22 +1168,34 @@
             gain_parts[i, 1:2, :] = gain_ffn[:, lanes]
             gain_parts[i, 2:8, :] = jnp.zeros((6, depth), F32)
         gain_deal.begin()
-        late.pump(pumps[7])
-        scatter_k.lines()
-        scatter_o.over()
+        query_g.hop(2)
+        key_g.hop(2)
+        scatter_o.line_step(0)
+        flow.pump(pumps[7])
+        context_s.cross()
+        branch_cols.rest()
+        branch_cols.times(context_all, grad_wo)
+
+        @pl.loop(3, nz)
+        def _(h):
+            query_g.hop(h)
+            key_g.hop(h)
+            scatter_o.line_step(h - 2)
+
+        flow.pump(pumps[8])
+        norm_cols.rest()
+        key_g.cross()
+        norm_cols.times(key_all, k_rows.at[t])
+        kv_g.begin()
         gain_land[d] = gain_parts[d]
         gain_deal.done()
         gain_sum[t] = jnp.sum(gain_land[...], axis=0)
         gain_g.begin()
-        scatter_k.total(acc_k)
-        k_rows[t] = acc_k[...]
-        kv_g.begin()
-        late.rest()
-        scatter_o.lines()
-        scatter_w.total(acc_w)
-        grad_wo[...] = acc_w[...]
-        scatter_q.total(acc_w)
-        grad_wq[...] = acc_w[...]
+        flow.rest()
+        scatter_o.line_step(nz - 2)
+        scatter_o.meet(net.z)
+        query_g.cross()
+        norm_cols.times(query_all, grad_wq)
         gain_g.rest()
         grad_gains[...] = jnp.sum(gain_sum[...], axis=0)
         kv_g.rest()
@@ -1103,16 +1203,11 @@
             grad_wkv[:, i * quarter : (i + 1) * quarter] = k_rows[i]
         scatter_o.total(acc)
         block_out[...] = (middle[...] + acc[...]).astype(BF16)
-        for end in ends:
-            end()
-
-    flow.rest()
+
+    assert net.used <= counts
     projection = pltpu.VMEM((features, heads), BF16)
     part = pltpu.VMEM((features, quarter), BF16)
-    pl.run_scoped(
-        attention, projection, projection, part, pltpu.VMEM((4 * rows, features), BF16),
-        projection, projection, part,
-    )
+    pl.run_scoped(attention, projection, projection, part)
     for deal in deals:
         deal.done()
     for copy in copies:
@@ -1126,8 +1221,8 @@
     )
 
 
-PUMPS_1 = (0.12, 0.1, 0.1, 0.1, 0.06, 0.1, 0.1, 0.1, 0.1, 0.12)
-PUMPS_2 = (1.0, 0.0, 0.2, 0.2, 0.1, 0.1, 0.2, 0.2)
+PUMPS_1 = (0.119, 0.0, 0.048, 0.048, 0.048, 0.048, 0.048, 0.095, 0.095, 0.095, 0.095, 0.095, 0.167, 0.0, 0.0, 0.0, 0.0, 0.0, 0.0)
+PUMPS_2 = (0.452, 0.0, 0.024, 0.19, 0.143, 0.095, 0.095, 0.0, 0.0, 0.0)
 
 
 def body(
@@ -1198,7 +1293,7 @@
 
     staged = n > 8
     subs = nz // tile_blocks
-    counts = 2 * (4 * subs + 5 * nz) + 3 * 3 * nz + 15 + n + 3 * parts * n
+    counts = 2 * (4 * subs + 5 * nz) + 3 * 3 * nz + 21 + 3 * n + 3 * parts * n
     landing = [
         shape((4, nz, rows, features), BF16),
         shape((2, nz, rows, features), BF16),
@@ -1224,22 +1319,16 @@
     else:
         in_vmem = [pltpu.VMEM(place.shape, place.dtype) for place in landing]
 
-    def reduced(columns):
-        return [
-            pltpu.VMEM((nz, depth, columns), BF16),
-            pltpu.VMEM((nz + 1, depth, columns), BF16),
-        ]
-
     results = pl.pallas_call(
         functools.partial(second_kernel, n, counts, staged, PUMPS_2),
         out_shape=tuple(out_shape),
-        in_specs=[SMEM, ANY, ANY, VMEM] + [ANY] * 10 + [VMEM] * 7,
+        in_specs=[SMEM] + [ANY] * 13 + [VMEM] * 7,
         out_specs=tuple(out_specs),
         scratch_shapes=in_vmem
         + [
             pltpu.SemaphoreType.DMA((counts,)),
             pltpu.SemaphoreType.DMA((counts,)),
-            pltpu.SemaphoreType.DMA((14,)),
+            pltpu.SemaphoreType.DMA((15,)),
             pltpu.VMEM((tile_blocks if staged else 1, rows, features), BF16),
             pltpu.VMEM((3, features, cut if parts > 1 else 128), BF16),
             pltpu.VMEM((rows, features), F32),
@@ -1251,18 +1340,20 @@
             pltpu.VMEM((2, rows, features), BF16),
             pltpu.VMEM((rows, features), BF16),
         ]
-        + reduced(heads)
-        + reduced(heads)
-        + reduced(quarter)
         + [
+            pltpu.VMEM((n * group_rows, heads), BF16),
+            pltpu.VMEM((n * group_rows, heads), BF16),
+            pltpu.VMEM((n * group_rows, quarter), BF16),
+            pltpu.VMEM((n, rows, depth), BF16),
+            pltpu.VMEM((4, n, rows, depth), BF16),
+            pltpu.VMEM((n, rows, depth), BF16),
+            pltpu.VMEM((4, n, rows, depth), BF16),
             pltpu.VMEM((4, depth, quarter), F32),
-            pltpu.VMEM((depth, heads), F32),
-            pltpu.VMEM((depth, quarter), F32),
             pltpu.VMEM((n, 8, depth), F32),
             pltpu.VMEM((n, 8, depth), F32),
             pltpu.VMEM((4, 8, depth), F32),
             pltpu.VMEM((group_rows, heads), BF16),
-            pltpu.VMEM((rows, features), F32),
+            pltpu.VMEM((rows, features), BF16),
         ],
         compiler_params=params(1),
         name="backward",

time: 520 us -> 463 us (0.89); the launches traced: 519 us -> 456 us
  Pallas kernels: 502 us -> 439 us
    pallas_call x1, Pallas kernels: 266 us -> 219 us  [body(): pl.pallas_call(functools.partial(second_kernel, n, counts, staged, PUMPS_...]
    pallas_call x1, Pallas kernels: 236 us -> 220 us  [body(): pl.pallas_call(functools.partial(first_kernel, n, counts, PUMPS_1), out_s...]
where the time goes in v3:
time: 463 us; the launch traced here: 456 us
  Pallas kernels  439 us (95%)
  other arithmetic  9.92 us (2%)
  local copies, waits for them, and re-layouts  6.64 us (1%)
    pallas_call x1, Pallas kernels, body(): pl.pallas_call(functools.partial(first_kernel, n, counts, PUMPS_1), out_s...  220 us
    pallas_call x1, Pallas kernels, body(): pl.pallas_call(functools.partial(second_kernel, n, counts, staged, PUMPS_...  219 us

profile of v3, /device:TPU:0, one launch (start us, length us, event | category | flops | bytes accessed | tf_op | source)
XLA Modules:
  0.0 456.4 jit_solution(4082506896599860513)
XLA Ops:
  0.7 0.1 pad.2.clone
  0.7 0.7 broadcast_in_dim.9
  1.4 0.7 broadcast_in_dim.10
  2.0 0.7 maximum_convert_fusion.gains
  2.7 220.3 %forward.1 = (bf16[2048,512]{1,0:T(8,128)(2,1)}, bf16[2048,512]{1,0:T(8,128)(2,1)}, bf16[2048,512]{1,0:T(8,128)(2,1)}, bf16[8,4,64,2048]{3,2,1,0:T(8,128)(2,1)},...) custom-call(s32[1,3]{1,0:T(1,128)} %lens.3, ...), custom_call_target="tpu_custom_call" | custom-call | tf_op jit(solution)/shard_map/forward/pallas_call | solution.py:1253
  223.0 218.9 %backward.1 = (bf16[64,2048]{1,0:T(8,128)(2,1)}, f32[64,2048]{1,0:T(8,128)}, f32[8,256]{1,0:T(8,128)}, f32[256,512]{1,0:T(8,128)}, f32[256,512]{1,0:T(8,128)}, /...) custom-call(s32[1,3]{1,0:T(1,128)} %lens.3, ...), custom_call_target="tpu_custom_call" | custom-call | tf_op jit(solution)/shard_map/backward/pallas_call | solution.py:1322
  441.9 1.3 fusion
  443.2 0.0 copy-start.1
  443.2 4.2 convert_element_type.13
  447.5 0.0 copy-done.1
  447.5 0.0 copy-start
  447.5 2.5 convert_element_type.14
  450.0 0.0 copy-done
  450.0 0.0 copy-start.6
  450.0 0.0 copy-start.5
  450.0 0.0 copy-start.4
  450.0 2.5 convert_element_type.15
  452.5 0.0 copy-done.6
  452.5 0.0 copy-start.3
  452.5 0.0 copy-start.2
  452.5 0.7 copy.26
  453.2 0.0 copy-done.5
  453.2 0.8 copy.27
  454.0 0.0 copy-done.4
  454.0 0.8 copy.28
  454.8 0.0 copy-done.3
  454.8 0.8 copy.29
  455.6 0.0 copy-done.2
  455.6 0.8 copy.30
  (1 shorter events, 0.0 us)
Async XLA Ops:
  443.2 4.3 copy-start.1
  447.5 2.5 copy-start
  450.0 2.5 copy-start.6
  450.0 3.2 copy-start.5
  450.0 4.0 copy-start.4
  452.5 2.3 copy-start.3
  452.5 3.1 copy-start.2

commit v4 on v3

--- a/solution.py
+++ b/solution.py
@@ -688,7 +688,8 @@
     n, counts, pumps,
     lens, tok, go, gains, wq, wkv, wo, wg, wu, wd,
     wg_all, wu_all, wd_all, x_all, g_all, wq_out, wkv_out, wo_out, gains_out,
-    query_out, keyval_out, context_out, normed_out, middle_out, acts_out, dwg_out, dwu_out, dwd_out,
+    query_hbm, keyval_hbm, context_hbm, normed_hbm, middle_hbm, acts_hbm, dwg_hbm, dwu_hbm, dwd_hbm,
+    query_out, keyval_out, context_out, normed_out, middle_out, acts_out, dw_out,
     send, recv, local, wq_all, wkv_all, wo_all, gains_all,
     group, kv_parts, branch, branch_c, branch_y, own_normed,
     w_part, x_tile, g_tile, acc_g, acc_u, acc_d,
@@ -735,7 +736,8 @@
         for w, full in ((wg, wg_all), (wu, wu_all), (wd, wd_all))
     ]
     own_copies = [
-        pltpu.make_async_copy(a, b, local.at[i]) for i, (a, b) in enumerate(own_copies)
+        pltpu.make_async_copy(a, b, local.at[i if i < 6 else 8 + i])
+        for i, (a, b) in enumerate(own_copies)
     ]
     for copy in own_copies:
         copy.start()
@@ -806,6 +808,11 @@
                 (wkv_all, wkv_out),
                 (wo_all, wo_out),
                 (gains_all, gains_out),
+                (query_out, query_hbm),
+                (keyval_out, keyval_hbm),
+                (context_out, context_hbm),
+                (normed_out, normed_hbm),
+                (middle_out, middle_hbm),
             )
         )
     ]
@@ -832,11 +839,11 @@
     ):
         copy.wait()
         deal.done()
-        pltpu.make_async_copy(full.at[:, pl.ds(0, cut)], w_part.at[i], local.at[5 + i]).start()
+        pltpu.make_async_copy(full.at[:, pl.ds(0, cut)], w_part.at[i], local.at[14 + i]).start()
     for acc in (acc_g, acc_u, acc_d):
         acc[...] = jnp.zeros_like(acc)
     for i, full in enumerate((wg_all, wu_all, wd_all)):
-        pltpu.make_async_copy(full.at[:, pl.ds(0, cut)], w_part.at[i], local.at[5 + i]).wait()
+        pltpu.make_async_copy(full.at[:, pl.ds(0, cut)], w_part.at[i], local.at[14 + i]).wait()
     flow.pump(pumps[11])
     tile_blocks = x_tile.shape[0]
     tile = tile_blocks * rows
@@ -867,7 +874,7 @@
         def _(sub):
             part = pl.ds(sub * tile_blocks, tile_blocks)
             loads = [
-                pltpu.make_async_copy(a.at[slot, part], b, local.at[5 + i])
+                pltpu.make_async_copy(a.at[slot, part], b, local.at[14 + i])
                 for i, (a, b) in enumerate(((x_all, x_tile), (g_all, g_tile)))
             ]
             for load in loads:
@@ -885,13 +892,16 @@
             acc_u[...] += dot_tn(x, grad_up)
             acc_d[...] += dot_tn(g, hidden)
 
-    dwg_out[...] = acc_g[...].astype(BF16)
-    dwu_out[...] = acc_u[...].astype(BF16)
-    dwd_out[...] = acc_d[...].astype(BF16)
     flow.rest()
+    more_outs = [pltpu.make_async_copy(acts_out, acts_hbm, local.at[10])]
+    for i, (total, place) in enumerate(((acc_g, dwg_hbm), (acc_u, dwu_hbm), (acc_d, dwd_hbm))):
+        dw_out[i] = total[...].astype(BF16)
+        more_outs.append(pltpu.make_async_copy(dw_out.at[i], place, local.at[11 + i]))
+    for copy in more_outs:
+        copy.start()
     for deal in deals[3:]:
         deal.done()
-    for copy in outs:
+    for copy in outs + more_outs:
         copy.wait()
     net.finish()
 
@@ -969,11 +979,6 @@
     )
     own_rows.start()
     block(context_all, d)[...] = context[...]
-    net.greet()
-    context_s.begin()
-    own_rows.wait()
-    norm_cols.begin(normed_own[...])
-    flow.pump(pumps[0], first_half)
 
     def ffn(wg_v, wu_v, wd_v, acts, x_tiles, g_tiles, x_cols, g_cols, one):
         w_loads = [
@@ -1027,6 +1032,11 @@
         if two:
             for load in loads(0):
                 load.start()
+        net.greet()
+        context_s.begin()
+        own_rows.wait()
+        norm_cols.begin(normed_own[...])
+        flow.pump(pumps[0], first_half)
         for load in w_loads:
             load.wait()
         more = slice(cut, width)
@@ -1215,6 +1225,16 @@
     net.finish()
 
 
+def finish_kernel(wg, wu, wd, tokens, wq, wkv, wo, block, wg_o, wu_o, wd_o, tokens_o, wq_o, wkv_o, wo_o, block_o):
+    for a, b in ((wg, wg_o), (wu, wu_o), (wd, wd_o)):
+        b[...] = a[...].astype(F32)
+
+    @pl.when(pl.program_id(0) == 0)
+    def _():
+        for a, b in ((tokens, tokens_o), (wq, wq_o), (wkv, wkv_o), (wo, wo_o), (block, block_o)):
+            b[...] = a[...]
+
+
 def params(collective_id):
     return pltpu.CompilerParams(
         collective_id=collective_id, has_side_effects=True, vmem_limit_bytes=63 * MIB
@@ -1267,11 +1287,18 @@
             part, part, part,
         ),
         in_specs=[SMEM] + [ANY] * 9,
-        out_specs=(ANY,) * 9 + (VMEM,) * 9,
+        out_specs=(ANY,) * 18,
         scratch_shapes=[
+            pltpu.VMEM((group_rows, heads), BF16),
+            pltpu.VMEM((group_rows, 2 * HD), BF16),
+            pltpu.VMEM((group_rows, heads), BF16),
+            pltpu.VMEM((group_rows, features), BF16),
+            pltpu.VMEM((rows, features), F32),
+            pltpu.VMEM((3, all_rows, cut), BF16),
+            pltpu.VMEM((3, features, cut), BF16),
             pltpu.SemaphoreType.DMA((counts,)),
             pltpu.SemaphoreType.DMA((counts,)),
-            pltpu.SemaphoreType.DMA((9,)),
+            pltpu.SemaphoreType.DMA((17,)),
             pltpu.VMEM((features, heads), BF16),
             pltpu.VMEM((features, quarter), BF16),
             pltpu.VMEM((features, heads), BF16),
@@ -1365,6 +1392,23 @@
     block_out, grad_tokens, grad_gains, grad_wq, grad_wkv, grad_wo, grad_wg, grad_wu, grad_wd = (
         results[:9]
     )
+    chunks = 4
+    column_block = pl.BlockSpec((depth, n * width // chunks), lambda i: (0, i))
+    small = [
+        pl.BlockSpec(a.shape, lambda i: (0, 0)) for a in (grad_tokens, grad_wq, grad_wkv, grad_wo, block_out)
+    ]
+    grad_wg, grad_wu, grad_wd, grad_tokens, grad_wq, grad_wkv, grad_wo, block_out = pl.pallas_call(
+        finish_kernel,
+        grid=(chunks,),
+        out_shape=tuple(shape((depth, n * width), F32) for _ in range(3))
+        + tuple(
+            shape(a.shape, a.dtype) for a in (grad_tokens, grad_wq, grad_wkv, grad_wo, block_out)
+        ),
+        in_specs=[column_block] * 3 + small,
+        out_specs=[column_block] * 3 + small,
+        compiler_params=pltpu.CompilerParams(vmem_limit_bytes=48 * MIB),
+        name="results",
+    )(grad_wg, grad_wu, grad_wd, grad_tokens, grad_wq, grad_wkv, grad_wo, block_out)
     return (
         block_out,
         grad_tokens,
@@ -1373,9 +1417,9 @@
         grad_wq,
         grad_wkv,
         grad_wo,
-        grad_wg.astype(F32),
-        grad_wu.astype(F32),
-        grad_wd.astype(F32),
+        grad_wg,
+        grad_wu,
+        grad_wd,
     )
 
 

time: 463 us -> 461 us (level)
  other arithmetic: 9.92 us -> 0.67 us
  Pallas kernels: 439 us -> 445 us
    convert_element_type x3 -> x0, other arithmetic: 9.25 us -> none  [the longest x1 4.25 us: body(): grad_wg.astype(F32)]
    pallas_call x0 -> x1, Pallas kernels: none -> 7.89 us  [body(): pl.pallas_call(finish_kernel, grid=(chunks,), out_shape=tuple((shape((dep...]
where the time goes in v4:
time: 461 us; the launch traced here: 456 us
  Pallas kernels  445 us (97%)
  local copies, waits for them, and re-layouts  9.44 us (2%)
    pallas_call x1, Pallas kernels, body(): pl.pallas_call(functools.partial(second_kernel, n, counts, staged, PUMPS_...  220 us
    pallas_call x1, Pallas kernels, body(): pl.pallas_call(functools.partial(first_kernel, n, counts, PUMPS_1), out_s...  217 us

profile of v4, /device:TPU:0, one launch (start us, length us, event | category | flops | bytes accessed | tf_op | source)
XLA Modules:
  0.0 456.1 jit_solution(4494384211082867164)
XLA Ops:
  0.7 0.1 pad.2.clone
  0.7 0.7 broadcast_in_dim.9
  1.4 0.7 broadcast_in_dim.10
  2.0 0.7 maximum_convert_fusion.gains
  2.7 217.0 %forward.1 = (bf16[2048,512]{1,0:T(8,128)(2,1)}, bf16[2048,512]{1,0:T(8,128)(2,1)}, bf16[2048,512]{1,0:T(8,128)(2,1)}, bf16[8,4,64,2048]{3,2,1,0:T(8,128)(2,1)},...) custom-call(s32[1,3]{1,0:T(1,128)} %lens.3, ...), custom_call_target="tpu_custom_call" | custom-call | tf_op jit(solution)/shard_map/forward/pallas_call | solution.py:1273
  219.7 220.2 %backward.1 = (bf16[64,2048]{1,0:T(8,128)(2,1)}, f32[64,2048]{1,0:T(8,128)}, f32[8,256]{1,0:T(8,128)}, f32[256,512]{1,0:T(8,128)}, f32[256,512]{1,0:T(8,128)}, /...) custom-call(s32[1,3]{1,0:T(1,128)} %lens.3, ...), custom_call_target="tpu_custom_call" | custom-call | tf_op jit(solution)/shard_map/backward/pallas_call | solution.py:1349
  440.0 1.3 fusion
  441.3 0.0 copy-start
  441.3 1.6 copy-done
  442.9 0.0 copy-start.1
  442.9 1.0 copy-done.1
  444.0 0.0 copy-start.2
  444.0 1.0 copy-done.2
  445.0 0.0 copy-start.3
  445.0 1.0 copy-done.3
  446.0 0.0 copy-start.4
  446.0 1.0 copy-done.4
  447.1 0.0 copy-start.5
  447.1 0.9 copy-done.5
  448.0 7.9 %results.1 = (f32[256,4096]{1,0:T(8,128)}, f32[256,4096]{1,0:T(8,128)}, f32[256,4096]{1,0:T(8,128)}, f32[64,2048]{1,0:T(8,128)}, f32[256,512]{1,0:T(8,128)}, /*i...) custom-call(bf16[256,4096]{1,0:T(8,128)(2,1)S(1)} %copy-done, ...), custom_call_target="tpu_custom_call" | custom-call | tf_op jit(solution)/shard_map/results/pallas_call | solution.py:1400
  (1 shorter events, 0.0 us)
Async XLA Ops:
  441.3 1.6 copy-start
  442.9 1.0 copy-start.1
  444.0 1.0 copy-start.2
  445.0 1.0 copy-start.3
  446.0 1.0 copy-start.4
  447.1 0.9 copy-start.5

commit v5 on v4

--- a/solution.py
+++ b/solution.py
@@ -75,6 +75,14 @@
     def sent(self, ref, k):
         self.make(ref, ref, k, self.tensor(self.tc)).wait_send()
 
+    def pair(self, m):
+        other, bit = 0, 1
+        while bit < self.n:
+            low, mask = (self.d // bit) % 2, (m // bit) % 2
+            other = other + bit * (low + mask - 2 * low * mask)
+            bit *= 2
+        return other
+
     def greet(self):
         barrier = pltpu.get_barrier_semaphore()
 
@@ -341,7 +349,7 @@
 
     def send(self, m):
         net = self.net
-        to = (net.d + m) % net.n
+        to = net.pair(m)
         net.start(self.src(to), self.dst(net.d), self.k + m, net.dp(to))
 
     def begin(self):
@@ -352,7 +360,7 @@
 
         @pl.loop(1, net.n)
         def _(m):
-            net.landed(self.dst((net.d - m + net.n) % net.n), self.k + m)
+            net.landed(self.dst(net.pair(m)), self.k + m)
 
     def end(self):
         net = self.net
@@ -363,11 +371,11 @@
 
 
 class Flow:
-    def __init__(self, n, groups, even_first):
+    def __init__(self, n, groups, key):
         self.todo = []
         for deals in groups:
-            for parity in (0, 1) if even_first else (1, 0):
-                self.todo += [(deal, m) for deal in deals for m in range(1, n) if m % 2 == parity]
+            pairs = sorted(range(1, n), key=key)
+            self.todo += [(deal, m) for deal in deals for m in pairs]
         self.gone, self.share = 0, 0.0
 
     def pump(self, share, limit=None):
@@ -686,7 +694,7 @@
 
 def first_kernel(
     n, counts, pumps,
-    lens, tok, go, gains, wq, wkv, wo, wg, wu, wd,
+    lens, tok, go, gain_attn, gain_ffn, wq, wkv, wo, wg, wu, wd,
     wg_all, wu_all, wd_all, x_all, g_all, wq_out, wkv_out, wo_out, gains_out,
     query_hbm, keyval_hbm, context_hbm, normed_hbm, middle_hbm, acts_hbm, dwg_hbm, dwu_hbm, dwd_hbm,
     query_out, keyval_out, context_out, normed_out, middle_out, acts_out, dw_out,
@@ -722,13 +730,16 @@
         for w, full in ((wg, wg_all), (wu, wu_all), (wd, wd_all))
     ]
     assert net.used <= counts
-    flow = Flow(n, [deals[:3], deals[3:]], True)
-
+    flow = Flow(n, [deals[:3], deals[3:]], KEY_1)
+
+    own_gains = block(gains_all, d)
+    own_gains[...] = jnp.zeros(own_gains.shape, F32)
+    own_gains[0:1, :] = gain_attn[...].astype(F32).reshape(1, -1)
+    own_gains[1:2, :] = gain_ffn[...].astype(F32).reshape(1, -1)
     own_copies = [
         (tok, group.at[t]),
         (wq, block(wq_all, d)),
         (wkv_own, block(wkv_all, d)),
-        (gains, block(gains_all, d)),
         (wo, block(wo_all, d)),
         (go, g_all.at[0, net.z]),
     ] + [
@@ -736,20 +747,20 @@
         for w, full in ((wg, wg_all), (wu, wu_all), (wd, wd_all))
     ]
     own_copies = [
-        pltpu.make_async_copy(a, b, local.at[i if i < 6 else 8 + i])
+        pltpu.make_async_copy(a, b, local.at[i if i < 5 else 9 + i])
         for i, (a, b) in enumerate(own_copies)
     ]
     for copy in own_copies:
         copy.start()
     net.greet()
 
-    for copy in own_copies[:4]:
+    for copy in own_copies[:3]:
         copy.wait()
     tokens_g.begin()
     first_w.begin()
     flow.pump(pumps[0])
+    own_copies[3].wait()
     own_copies[4].wait()
-    own_copies[5].wait()
     tokens_g.rest()
     second_w.begin()
     spread_g.begin(go)
@@ -835,7 +846,7 @@
         spread_g.core_done(slot)
 
     for i, (copy, deal, full) in enumerate(
-        zip(own_copies[6:], deals[:3], (wg_all, wu_all, wd_all))
+        zip(own_copies[5:], deals[:3], (wg_all, wu_all, wd_all))
     ):
         copy.wait()
         deal.done()
@@ -966,7 +977,7 @@
             )
             for i, out in enumerate(outs)
         ]
-    flow = Flow(n, [deals[:3], deals[3:]], False)
+    flow = Flow(n, [deals[:3], deals[3:]], KEY_2)
     first_half = 3 * (n - 1)
     copies = [
         pltpu.make_async_copy(deal.src(d), deal.dst(d), local.at[1 + i])
@@ -1225,7 +1236,10 @@
     net.finish()
 
 
-def finish_kernel(wg, wu, wd, tokens, wq, wkv, wo, block, wg_o, wu_o, wd_o, tokens_o, wq_o, wkv_o, wo_o, block_o):
+def finish_kernel(
+    wg, wu, wd, tokens, wq, wkv, wo, block, gains,
+    wg_o, wu_o, wd_o, tokens_o, wq_o, wkv_o, wo_o, block_o, gain_attn_o, gain_ffn_o,
+):
     for a, b in ((wg, wg_o), (wu, wu_o), (wd, wd_o)):
         b[...] = a[...].astype(F32)
 
@@ -1233,6 +1247,8 @@
     def _():
         for a, b in ((tokens, tokens_o), (wq, wq_o), (wkv, wkv_o), (wo, wo_o), (block, block_o)):
             b[...] = a[...]
+        gain_attn_o[...] = gains[0:1, :]
+        gain_ffn_o[...] = gains[1:2, :]
 
 
 def params(collective_id):
@@ -1241,6 +1257,8 @@
     )
 
 
+KEY_1 = lambda m: -m
+KEY_2 = lambda m: (1 - m % 2, m)
 PUMPS_1 = (0.119, 0.0, 0.048, 0.048, 0.048, 0.048, 0.048, 0.095, 0.095, 0.095, 0.095, 0.095, 0.167, 0.0, 0.0, 0.0, 0.0, 0.0, 0.0)
 PUMPS_2 = (0.452, 0.0, 0.024, 0.19, 0.143, 0.095, 0.095, 0.0, 0.0, 0.0)
 
@@ -1255,10 +1273,6 @@
     width = w_gate.shape[1] // n
     group_rows = 4 * rows
     shape = jax.ShapeDtypeStruct
-    gains = jnp.concatenate(
-        [gain_attn[None], gain_ffn[None], jnp.zeros((6, depth), gain_attn.dtype)]
-    ).astype(F32)
-
     cut = width // 2 if width // 2 % 128 == 0 else width
     parts = width // cut
     tile_blocks = 256 // rows
@@ -1286,7 +1300,7 @@
             shape((3, all_rows, cut), BF16),
             part, part, part,
         ),
-        in_specs=[SMEM] + [ANY] * 9,
+        in_specs=[SMEM, ANY, ANY, VMEM, VMEM] + [ANY] * 6,
         out_specs=(ANY,) * 18,
         scratch_shapes=[
             pltpu.VMEM((group_rows, heads), BF16),
@@ -1316,7 +1330,8 @@
         + [pltpu.VMEM((features, cut), F32)] * 3,
         compiler_params=params(0),
         name="forward",
-    )(lengths, tokens, grad_out, gains, w_query, w_keyval, w_out, w_gate, w_up, w_down)
+    )(
+        lengths, tokens, grad_out, gain_attn, gain_ffn, w_query, w_keyval, w_out, w_gate, w_up, w_down)
 
     staged = n > 8
     subs = nz // tile_blocks
@@ -1392,28 +1407,33 @@
     block_out, grad_tokens, grad_gains, grad_wq, grad_wkv, grad_wo, grad_wg, grad_wu, grad_wd = (
         results[:9]
     )
-    chunks = 4
+    chunks = 2
     column_block = pl.BlockSpec((depth, n * width // chunks), lambda i: (0, i))
     small = [
         pl.BlockSpec(a.shape, lambda i: (0, 0)) for a in (grad_tokens, grad_wq, grad_wkv, grad_wo, block_out)
     ]
-    grad_wg, grad_wu, grad_wd, grad_tokens, grad_wq, grad_wkv, grad_wo, block_out = pl.pallas_call(
+    gain_spec = pl.BlockSpec((1, depth), lambda i: (0, 0))
+    (
+        grad_wg, grad_wu, grad_wd, grad_tokens, grad_wq, grad_wkv, grad_wo, block_out,
+        grad_gain_attn, grad_gain_ffn,
+    ) = pl.pallas_call(
         finish_kernel,
         grid=(chunks,),
         out_shape=tuple(shape((depth, n * width), F32) for _ in range(3))
         + tuple(
             shape(a.shape, a.dtype) for a in (grad_tokens, grad_wq, grad_wkv, grad_wo, block_out)
-        ),
-        in_specs=[column_block] * 3 + small,
-        out_specs=[column_block] * 3 + small,
-        compiler_params=pltpu.CompilerParams(vmem_limit_bytes=48 * MIB),
+        )
+        + (shape((1, depth), F32),) * 2,
+        in_specs=[column_block] * 3 + small + [pl.BlockSpec((8, depth), lambda i: (0, 0))],
+        out_specs=[column_block] * 3 + small + [gain_spec] * 2,
+        compiler_params=pltpu.CompilerParams(vmem_limit_bytes=63 * MIB),
         name="results",
-    )(grad_wg, grad_wu, grad_wd, grad_tokens, grad_wq, grad_wkv, grad_wo, block_out)
+    )(grad_wg, grad_wu, grad_wd, grad_tokens, grad_wq, grad_wkv, grad_wo, block_out, grad_gains)
     return (
         block_out,
         grad_tokens,
-        grad_gains[0],
-        grad_gains[1],
+        grad_gain_attn.reshape(depth),
+        grad_gain_ffn.reshape(depth),
         grad_wq,
         grad_wkv,
         grad_wo,

time: 461 us -> 452 us (0.980)
  local copies, waits for them, and re-layouts: 9.44 us -> 0 us
    unnamed x12 -> x0, local copies, waits for them, and re-layouts: 6.7 us -> none
    pallas_call x1, Pallas kernels: 220 us -> 226 us  [body(): pl.pallas_call(functools.partial(second_kernel, n, counts, staged, PUMPS_...]
    pallas_call x1, Pallas kernels: 217 us -> 212 us  [body(): pl.pallas_call(functools.partial(first_kernel, n, counts, PUMPS_1), out_s...]
where the time goes in v5:
time: 452 us; the launch traced here: 447 us
  Pallas kernels  446 us (99%)
    pallas_call x1, Pallas kernels, body(): pl.pallas_call(functools.partial(second_kernel, n, counts, staged, PUMPS_...  226 us
    pallas_call x1, Pallas kernels, body(): pl.pallas_call(functools.partial(first_kernel, n, counts, PUMPS_1), out_s...  212 us

profile of v5, /device:TPU:0, one launch (start us, length us, event | category | flops | bytes accessed | tf_op | source)
XLA Modules:
  0.0 447.2 jit_solution(1142024365269847081)
XLA Ops:
  0.6 212.0 %forward.1 = (bf16[2048,512]{1,0:T(8,128)(2,1)}, bf16[2048,512]{1,0:T(8,128)(2,1)}, bf16[2048,512]{1,0:T(8,128)(2,1)}, bf16[8,4,64,2048]{3,2,1,0:T(8,128)(2,1)},...) custom-call(s32[1,3]{1,0:T(1,128)} %lens.3, ...), custom_call_target="tpu_custom_call" | custom-call | tf_op jit(solution)/shard_map/forward/pallas_call | solution.py:1287
  212.7 225.7 %backward.1 = (bf16[64,2048]{1,0:T(8,128)(2,1)}, f32[64,2048]{1,0:T(8,128)}, f32[8,256]{1,0:T(8,128)}, f32[256,512]{1,0:T(8,128)}, f32[256,512]{1,0:T(8,128)}, /...) custom-call(s32[1,3]{1,0:T(1,128)} %lens.3, ...), custom_call_target="tpu_custom_call" | custom-call | tf_op jit(solution)/shard_map/backward/pallas_call | solution.py:1364
  438.4 8.7 %results.1 = (f32[256,4096]{1,0:T(8,128)}, f32[256,4096]{1,0:T(8,128)}, f32[256,4096]{1,0:T(8,128)}, f32[64,2048]{1,0:T(8,128)}, f32[256,512]{1,0:T(8,128)}, /*i...) custom-call(bf16[256,4096]{1,0:T(8,128)(2,1)} %get-tuple-element.65., ...), custom_call_target="tpu_custom_call" | custom-call | tf_op jit(solution)/shard_map/results/pallas_call | solution.py:1419

commit v6 on v5

--- a/solution.py
+++ b/solution.py
@@ -1260,7 +1260,7 @@
 KEY_1 = lambda m: -m
 KEY_2 = lambda m: (1 - m % 2, m)
 PUMPS_1 = (0.119, 0.0, 0.048, 0.048, 0.048, 0.048, 0.048, 0.095, 0.095, 0.095, 0.095, 0.095, 0.167, 0.0, 0.0, 0.0, 0.0, 0.0, 0.0)
-PUMPS_2 = (0.452, 0.0, 0.024, 0.19, 0.143, 0.095, 0.095, 0.0, 0.0, 0.0)
+PUMPS_2 = (0.476, 0.0, 0.024, 0.238, 0.119, 0.071, 0.071, 0.0, 0.0, 0.0)
 
 
 def body(

time: 452 us -> 450 us (level)
  no operation moved by 1% of the time
where the time goes in v6:
time: 450 us; the launch traced here: 446 us
  Pallas kernels  445 us (99%)
    pallas_call x1, Pallas kernels, body(): pl.pallas_call(functools.partial(second_kernel, n, counts, staged, PUMPS_...  225 us
    pallas_call x1, Pallas kernels, body(): pl.pallas_call(functools.partial(first_kernel, n, counts, PUMPS_1), out_s...  212 us

profile of v6, /device:TPU:0, one launch (start us, length us, event | category | flops | bytes accessed | tf_op | source)
XLA Modules:
  0.0 446.2 jit_solution(17432026827783198762)
XLA Ops:
  0.6 212.0 %forward.1 = (bf16[2048,512]{1,0:T(8,128)(2,1)}, bf16[2048,512]{1,0:T(8,128)(2,1)}, bf16[2048,512]{1,0:T(8,128)(2,1)}, bf16[8,4,64,2048]{3,2,1,0:T(8,128)(2,1)},...) custom-call(s32[1,3]{1,0:T(1,128)} %lens.3, ...), custom_call_target="tpu_custom_call" | custom-call | tf_op jit(solution)/shard_map/forward/pallas_call | solution.py:1287
  212.7 224.7 %backward.1 = (bf16[64,2048]{1,0:T(8,128)(2,1)}, f32[64,2048]{1,0:T(8,128)}, f32[8,256]{1,0:T(8,128)}, f32[256,512]{1,0:T(8,128)}, f32[256,512]{1,0:T(8,128)}, /...) custom-call(s32[1,3]{1,0:T(1,128)} %lens.3, ...), custom_call_target="tpu_custom_call" | custom-call | tf_op jit(solution)/shard_map/backward/pallas_call | solution.py:1364
  437.4 8.7 %results.1 = (f32[256,4096]{1,0:T(8,128)}, f32[256,4096]{1,0:T(8,128)}, f32[256,4096]{1,0:T(8,128)}, f32[64,2048]{1,0:T(8,128)}, f32[256,512]{1,0:T(8,128)}, /*i...) custom-call(bf16[256,4096]{1,0:T(8,128)(2,1)} %get-tuple-element.65., ...), custom_call_target="tpu_custom_call" | custom-call | tf_op jit(solution)/shard_map/results/pallas_call | solution.py:1419
